TPU v7x, 256 devices: a whole 4x4x8 slice. The times are simulated.
256 devices in a mesh: node: 32 (over z, y), feat: 8 (over x, core).
Axes of the slice: x: 4, y: 4, z: 8, core: 2. Of those that a mesh axis runs over, the one named last changes fastest.
Arguments:
- batch_node_input: bfloat16 [49152, 1024], P('node', 'feat'), may hold values from -6 to 6
- weight_in: bfloat16 [1024, 1024], P('feat'), may hold values from -0.1875 to 0.1875
- second_layer_weight: bfloat16 [1024, 1024], replicated, may hold values from -0.1875 to 0.1875
- send_rows: int32 [32, 32, 128], P('node'), may hold values from 0 to 1535
- recv_rows: int32 [32, 32, 128], P('node'), may hold values from 0 to 1535
- block_count: int32 [32, 32, 1], P('node'), may hold values from 16 to 128, as said below
Outputs:
- layer_two: bfloat16 [49152, 1024], P('node', 'feat')
Inputs may be any that keep to these rules, and one draw needn't show every extreme that they name: `block_count`: blocks from partition q to partition p hold their live rows first; the most live rows in a block is 128.
All inputs are finite; a program needn't handle non-finite values.
Results may differ from a plain program's by a relative error of at most 0.025.
Values may be sent and summed in bfloat16 or wider, within the bound.
A program may use at most 64 MiB of HBM per device.

v0:
```python
import jax
import jax.numpy as jnp
from jax import lax
from jax.sharding import PartitionSpec as P


def aggregate(dense_matrix, selection_lookup, neighbour_sum_lookup, degree):
    outgoing = jnp.einsum(
        "kig,gl->kil", selection_lookup, dense_matrix, preferred_element_type=jnp.float32
    ).astype(jnp.bfloat16)
    incoming = lax.all_to_all(outgoing, "node", split_axis=0, concat_axis=0, tiled=True)
    flat = incoming.reshape(-1, dense_matrix.shape[1])
    total = dense_matrix.astype(jnp.float32) + jnp.dot(
        neighbour_sum_lookup, flat, preferred_element_type=jnp.float32
    )
    return total / degree[:, None]


def per_device(batch_node_input, weight_in, second_layer_weight, send_rows, recv_rows, block_count):
    nfeat = lax.axis_size("feat")
    findex = lax.axis_index("feat")
    hidden_units = weight_in.shape[1]
    hid_slice = hidden_units // nfeat
    rows = batch_node_input.shape[0]
    block_rows = recv_rows.shape[2] // block_count.shape[2]
    row_ids = jnp.arange(rows, dtype=jnp.int32)
    outbound_local_rows = send_rows[0]
    selection_lookup = (outbound_local_rows[:, :, None] == row_ids[None, None, :]).astype(
        jnp.bfloat16
    )
    target_nodes = recv_rows[0].reshape(-1)
    live = (
        jnp.arange(block_rows, dtype=jnp.int32)[None, None, :] < block_count[0][..., None]
    ).reshape(-1)
    neighbour_sum_lookup = ((row_ids[:, None] == target_nodes[None, :]) & live[None, :]).astype(
        jnp.bfloat16
    )
    degree = 1.0 + jnp.sum(neighbour_sum_lookup, axis=1, dtype=jnp.float32)
    term = jnp.dot(batch_node_input, weight_in, preferred_element_type=jnp.float32).astype(
        jnp.bfloat16
    )
    first = (
        lax.psum_scatter(term, "feat", scatter_dimension=1, tiled=True)
        .astype(jnp.float32)
        .astype(jnp.bfloat16)
    )
    hidden = jnp.maximum(
        aggregate(first, selection_lookup, neighbour_sum_lookup, degree), 0.0
    ).astype(jnp.bfloat16)
    my_rows = lax.dynamic_slice_in_dim(second_layer_weight, findex * hid_slice, hid_slice, 0)
    term_two = jnp.dot(hidden, my_rows, preferred_element_type=jnp.float32).astype(jnp.bfloat16)
    second = (
        lax.psum_scatter(term_two, "feat", scatter_dimension=1, tiled=True)
        .astype(jnp.float32)
        .astype(jnp.bfloat16)
    )
    return aggregate(second, selection_lookup, neighbour_sum_lookup, degree).astype(jnp.bfloat16)


def solution(mesh):
    in_specs = (
        P("node", "feat"),
        P("feat", None),
        P(),
        P("node", None, None),
        P("node", None, None),
        P("node", None, None),
    )
    out_specs = P("node", "feat")
    return jax.shard_map(
        per_device, mesh=mesh, in_specs=in_specs, out_specs=out_specs, check_vma=False
    )
```

profile of v0, /device:TPU:32, one launch (start us, length us, event | category | flops | bytes accessed | tf_op | source)
XLA Modules:
  0.0 201.9 jit_solution(9916034893562441045)
XLA Ops:
  6.5 0.0 copy-start
  6.5 0.0 reduce-scatter.7.cloned.1.call-start
  6.5 3.9 %convolution_convert_fusion.1 = bf16[1536,1024]{1,0:T(8,128)(2,1)} fusion(bf16[1536,128]{1,0:T(8,128)(2,1)} %param.6, bf16[128,1024]{1,0:T(8,128)(2,1)} %param.7), kind=kOutput, calls=%fused_computation.16 | convolution fusion | flops 404226048 | bytes 3801088 | tf_op jit(solution)/shard_map/dot_general | solution.py:39
  10.4 4.6 %copy.7 = bf16[1536,1024]{0,1:T(8,128)(2,1)} copy(bf16[1536,1024]{1,0:T(8,128)(2,1)} %convolution_convert_fusion.1) | data formatting | bytes 6291456
  15.0 0.0 copy-start.4
  15.0 0.0 reduce-scatter.7.cloned.1.call-update
  15.1 40.9 %reduce-scatter.7.cloned.1.call-done = bf16[128,1536]{1,0:T(8,128)(2,1)} async-done(((bf16[1024,1536]{1,0:T(8,128)(2,1)}), bf16[128,1536]{1,0:T(8,128)(2,1)}) %reduce-scatter.7.cloned.1.call-update) | async-done | bytes 393232
  56.0 0.0 copy-done.4
  56.0 0.0 copy-start.3
  56.0 0.0 copy-start.1
  56.0 6.5 %fusion.37 = bf16[32,128,128]{2,1,0:T(8,128)(2,1)} fusion(s32[32,128]{1,0:T(8,128)S(1)} %bitcast.32, bf16[128,1536]{1,0:T(8,128)(2,1)} %reduce-scatter.7.cloned.1.call-done), kind=kOutput, calls=%fused_computation.24 | convolution fusion | flops 1617428480 | bytes 1458176 | tf_op jit(solution)/shard_map/kig,gl->kil/dot_general | solution.py:8
  62.5 10.2 %all-to-all-start = ((bf16[32,128,128]{2,1,0:T(8,128)(2,1)}), bf16[32,128,128]{2,1,0:T(8,128)(2,1)S(1)}, u32[]{:S(2)}, u32[]{:S(2)}) async-start(bf16[32,128,128]{2,1,0:T(8,128)(2,1)} %fusion.37), calls=%async_computation | async-start | bytes 2097152 | tf_op jit(solution)/shard_map/all_to_all | solution.py:11
  72.7 0.2 reduce-scatter.9.cloned.1.call-start
  72.9 0.0 copy-done.3
  72.9 0.1 fusion.45
  73.0 5.9 %convert_reduce_fusion = f32[1536]{0:T(1024)S(1)} fusion(s32[4096]{0:T(1024)} %bitcast.34, pred[4096]{0:T(1024)(128)(4,1)S(1)} %fusion.45), kind=kLoop, calls=%fused_computation | loop fusion | flops 31455744 | bytes 26624 | tf_op jit(solution)/shard_map/reduce_sum | solution.py:38
  78.9 0.0 copy-done.1
  79.0 0.9 copy.8
  79.9 17.5 %all-to-all-done = bf16[32,128,128]{2,1,0:T(8,128)(2,1)S(1)} async-done(((bf16[32,128,128]{2,1,0:T(8,128)(2,1)}), bf16[32,128,128]{2,1,0:T(8,128)(2,1)S(1)}, u32[]{:S(2)}, u32[]{:S(2)}) %all-to-all-start) | async-done | bytes 1048608 | tf_op jit(solution)/shard_map/all_to_all | solution.py:11
  97.4 0.0 copy-done
  97.4 8.6 %convolution_convert_fusion = bf16[1536,1024]{1,0:T(8,128)(2,1)} fusion(bf16[4096,128]{1,0:T(8,128)(2,1)S(1)} %bitcast.27, s32[4096]{0:T(1024)} %bitcast.35, pred[4096]{0:T(1024)(128)(4,1)S(1)} %fusion.45, bf16[1536,128]{1,0:T(8,128)(2,1)} %copy.8, f32[1536]{0:T(1024)S(1)} %broadcast_add_fusion, bf16[1024,1024]{1,0:T(8,128)(2,1)S(1)} %copy-done, ...), kind=kOutput, calls=%fused_computation.15 | convolution fusion | flops 2028404736 | bytes 4878340 | tf_op jit(solution)/shard_map/dot_general | solution.py:51
  106.0 4.6 %copy.9 = bf16[1536,1024]{0,1:T(8,128)(2,1)} copy(bf16[1536,1024]{1,0:T(8,128)(2,1)} %convolution_convert_fusion) | data formatting | bytes 6291456
  110.6 0.0 copy-start.5
  110.6 0.0 reduce-scatter.9.cloned.1.call-update
  110.6 35.7 %reduce-scatter.9.cloned.1.call-done = bf16[128,1536]{1,0:T(8,128)(2,1)} async-done(((bf16[1024,1536]{1,0:T(8,128)(2,1)}), bf16[128,1536]{1,0:T(8,128)(2,1)}) %reduce-scatter.9.cloned.1.call-update) | async-done | bytes 393232
  146.4 0.0 copy-done.5
  146.4 6.5 %fusion.38 = bf16[32,128,128]{2,1,0:T(8,128)(2,1)} fusion(s32[32,128]{1,0:T(8,128)S(1)} %bitcast.33, bf16[128,1536]{1,0:T(8,128)(2,1)} %reduce-scatter.9.cloned.1.call-done), kind=kOutput, calls=%fused_computation.25 | convolution fusion | flops 1617428480 | bytes 1458176 | tf_op jit(solution)/shard_map/kig,gl->kil/dot_general | solution.py:8
  152.9 10.1 %all-to-all-start.1 = ((bf16[32,128,128]{2,1,0:T(8,128)(2,1)}), bf16[32,128,128]{2,1,0:T(8,128)(2,1)S(1)}, u32[]{:S(2)}, u32[]{:S(2)}) async-start(bf16[32,128,128]{2,1,0:T(8,128)(2,1)} %fusion.38), calls=%async_computation.1 | async-start | bytes 2097152 | tf_op jit(solution)/shard_map/all_to_all | solution.py:11
  163.0 0.0 copy-done.2
  163.0 0.9 copy.10
  164.0 23.7 %all-to-all-done.1 = bf16[32,128,128]{2,1,0:T(8,128)(2,1)S(1)} async-done(((bf16[32,128,128]{2,1,0:T(8,128)(2,1)}), bf16[32,128,128]{2,1,0:T(8,128)(2,1)S(1)}, u32[]{:S(2)}, u32[]{:S(2)}) %all-to-all-start.1) | async-done | bytes 1048608 | tf_op jit(solution)/shard_map/all_to_all | solution.py:11
  187.7 7.3 %fusion.23 = bf16[1536,128]{1,0:T(8,128)(2,1)} fusion(bf16[4096,128]{1,0:T(8,128)(2,1)S(1)} %bitcast.28, s32[4096]{0:T(1024)} %bitcast.36, pred[4096]{0:T(1024)(128)(4,1)S(1)} %fusion.45, bf16[1536,128]{1,0:T(8,128)(2,1)} %copy.10, f32[1536]{0:T(1024)S(1)} %broadcast_add_fusion), kind=kOutput, calls=%fused_computation.20 | convolution fusion | flops 1623982080 | bytes 1861632 | tf_op jit(solution)/shard_map/dot_general | solution.py:13
  (2 shorter events, 0.0 us)
Async XLA Ops:
  6.5 90.8 %copy-start = (bf16[1024,1024]{1,0:T(8,128)(2,1)S(1)}, bf16[1024,1024]{1,0:T(8,128)(2,1)}, u32[]{:S(2)}) copy-start(bf16[1024,1024]{1,0:T(8,128)(2,1)} %param.8) | copy-start | bytes 6291460
  6.5 49.5 %reduce-scatter.7.cloned.1.call-start = ((), (), s32[]{:S(2)}) async-start(), calls=%async_computation.4 | async-start | bytes 3538944
  15.0 41.0 %copy-start.4 = (s32[1,32,128]{2,1,0:T(8,128)S(1)}, s32[1,32,128]{2,1,0:T(8,128)}, u32[]{:S(2)}) copy-start(s32[1,32,128]{2,1,0:T(8,128)} %param.9) | copy-start | bytes 49156
  56.0 16.9 %copy-start.3 = (s32[1,32,1]{1,2,0:T(1,128)S(1)}, s32[1,32,1]{1,2,0:T(1,128)}, u32[]{:S(2)}) copy-start(s32[1,32,1]{1,2,0:T(1,128)} %param.11) | copy-start | bytes 388
  56.0 22.9 %copy-start.1 = (bf16[128,1536]{1,0:T(8,128)(2,1)S(1)}, bf16[128,1536]{1,0:T(8,128)(2,1)}, u32[]{:S(2)}) copy-start(bf16[128,1536]{1,0:T(8,128)(2,1)} %reduce-scatter.7.cloned.1.call-done) | copy-start | bytes 1179652
  62.5 34.8 %all-to-all-start = ((bf16[32,128,128]{2,1,0:T(8,128)(2,1)}), bf16[32,128,128]{2,1,0:T(8,128)(2,1)S(1)}, u32[]{:S(2)}, u32[]{:S(2)}) async-start(bf16[32,128,128]{2,1,0:T(8,128)(2,1)} %fusion.37), calls=%async_computation | async-start | bytes 2097152 | tf_op jit(solution)/shard_map/all_to_all | solution.py:11
  72.7 73.7 %reduce-scatter.9.cloned.1.call-start = ((), (), s32[]{:S(2)}) async-start(), calls=%async_computation.5 | async-start | bytes 3538944
  110.6 35.7 %copy-start.5 = (s32[1,32,128]{2,1,0:T(8,128)S(1)}, s32[1,32,128]{2,1,0:T(8,128)}, u32[]{:S(2)}) copy-start(s32[1,32,128]{2,1,0:T(8,128)} %param.9) | copy-start | bytes 49156
  146.4 16.7 %copy-start.2 = (bf16[128,1536]{1,0:T(8,128)(2,1)S(1)}, bf16[128,1536]{1,0:T(8,128)(2,1)}, u32[]{:S(2)}) copy-start(bf16[128,1536]{1,0:T(8,128)(2,1)} %reduce-scatter.9.cloned.1.call-done) | copy-start | bytes 1179652
  152.9 34.8 %all-to-all-start.1 = ((bf16[32,128,128]{2,1,0:T(8,128)(2,1)}), bf16[32,128,128]{2,1,0:T(8,128)(2,1)S(1)}, u32[]{:S(2)}, u32[]{:S(2)}) async-start(bf16[32,128,128]{2,1,0:T(8,128)(2,1)} %fusion.38), calls=%async_computation.1 | async-start | bytes 2097152 | tf_op jit(solution)/shard_map/all_to_all | solution.py:11
Sparse Core Ops, SparseCore 0:
  15.2 40.7 reduce-scatter.6
  110.8 35.5 reduce-scatter.8
where the time goes:
time: 204 us; the launch traced here: 202 us
  waiting for transfers between devices  118 us (58%)
  matrix products  32.8 us (16%)
  starting transfers between devices  20.5 us (10%)
  between operations  13.5 us (7%)
  local copies, waits for them, and re-layouts  11.1 us (5%)
  other arithmetic  6 us (3%)
    unnamed x4, waiting for transfers between devices  76.7 us
    all_to_all x2, waiting for transfers between devices, aggregate(): lax.all_to_all(outgoing, 'node', split_axis=0, concat_axis=0, tiled=True)  41.2 us
    all_to_all x2, starting transfers between devices, aggregate(): lax.all_to_all(outgoing, 'node', split_axis=0, concat_axis=0, tiled=True)  20.3 us
    dot_general x2, matrix products, aggregate(): jnp.einsum('kig,gl->kil', selection_lookup, dense_matrix, preferred_eleme...  13 us
    unnamed x16, local copies, waits for them, and re-layouts  11.1 us
    dot_general x1, matrix products, per_device(): jnp.dot(hidden, my_rows, preferred_element_type=jnp.float32)  8.62 us
    dot_general x1, matrix products, aggregate(): jnp.dot(neighbour_sum_lookup, flat, preferred_element_type=jnp.float32)  7.32 us
    reduce_sum x1, other arithmetic, per_device(): degree = 1.0 + jnp.sum(neighbour_sum_lookup, axis=1, dtype=jnp.float32)  5.92 us
  transfers between devices with their start and end apart: 4, of which 4 were waited for; matrix products, arithmetic and copies ran while one was open for 4% of the time, Pallas kernels for 0%

commit v1 on v0

v1 whole, which is shorter than its diff:
```python
import functools

import jax
import jax.numpy as jnp
from jax import lax
from jax.experimental import pallas as pl
from jax.experimental.pallas import tpu as pltpu
from jax.sharding import PartitionSpec as P

MESH = pl.DeviceIdType.MESH
NZ, NY, NX, NC = 8, 4, 4, 2
NODES, FEATS = NZ * NY, NX * NC
BF16, F32 = jnp.bfloat16, jnp.float32


def order(i):
    return lax.rem(4 + lax.rem(i, 2) * ((i + 1) // 2) - (1 - lax.rem(i, 2)) * (i // 2), NZ)


def kernel(
    x_ref, w1_ref, w2_hbm, send_ref, recv_ref, count_ref, out_ref,
    w1_all, w2_all, out_slots, in_slots, send_cols, recv_live, pick, place,
    total, degree, mine, rows_in, rows_out, second,
    slot_send, slot_recv, w1_send, w1_recv, w1_send2, w1_recv2, row_send, row_recv, w2_sem,
):
    rows, width = x_ref.shape
    slots = send_ref.shape[1]
    part = rows // FEATS
    node, feat = lax.axis_index("node"), lax.axis_index("feat")
    z, y = node // NY, lax.rem(node, NY)
    x, c = feat // NC, lax.rem(feat, NC)

    barrier = pltpu.get_barrier_semaphore()

    def greet_node(k, _):
        other = lax.rem(node + k, NODES)
        pl.semaphore_signal(barrier, inc=1, device_id=(other, feat), device_id_type=MESH)
        return 0

    def greet_feat(k, _):
        other = lax.rem(feat + k, FEATS)
        pl.semaphore_signal(barrier, inc=1, device_id=(node, other), device_id_type=MESH)
        return 0

    lax.fori_loop(1, FEATS, greet_feat, 0)
    lax.fori_loop(1, NODES, greet_node, 0)

    w2_copy = pltpu.make_async_copy(w2_hbm, w2_all, w2_sem)
    w2_copy.start()
    send_cols[...] = send_ref[...].astype(F32).T
    slot_id = lax.broadcasted_iota(jnp.int32, recv_ref.shape, 1)
    live = jnp.where(slot_id < count_ref[...], recv_ref[...], -1)
    for q in range(NZ):
        recv_live[q] = live[q * NY:(q + 1) * NY]
    w1_all[feat] = w1_ref[...]

    pl.semaphore_wait(barrier, NODES + FEATS - 2)

    def w1_copy(dx):
        return pltpu.make_async_remote_copy(
            w1_ref, w1_all.at[feat], w1_send.at[dx], w1_recv.at[dx],
            device_id=(node, lax.rem(x + dx, NX) * NC + c), device_id_type=MESH)

    def w1_pass(dx):
        held = lax.rem(x + NX - dx, NX) * NC + c
        return pltpu.make_async_remote_copy(
            w1_all.at[held], w1_all.at[held], w1_send2.at[dx], w1_recv2.at[dx],
            device_id=(node, x * NC + 1 - c), device_id_type=MESH)

    def slot_copy(layer, other):
        return pltpu.make_async_remote_copy(
            out_slots.at[layer, other], in_slots.at[layer, node],
            slot_send.at[layer, other], slot_recv.at[layer, node],
            device_id=(other, feat), device_id_type=MESH)

    def slot_wait(layer, other):
        pltpu.make_async_remote_copy(
            out_slots.at[layer, other], in_slots.at[layer, other],
            slot_send.at[layer, other], slot_recv.at[layer, other],
            device_id=(other, feat), device_id_type=MESH).wait_recv()

    def select(layer, source, zz):
        cols = send_cols[...]
        lane = lax.broadcasted_iota(jnp.int32, cols.shape, 1)
        row_id = lax.broadcasted_iota(jnp.int32, (slots, rows), 1).astype(F32)
        for j in range(NY):
            col = jnp.sum(jnp.where(lane == zz * NY + j, cols, 0.0), axis=1, keepdims=True)
            pick[j * slots:(j + 1) * slots, :] = jnp.where(row_id == col, 1.0, 0.0).astype(BF16)
        got = jnp.dot(pick[...], source[...], preferred_element_type=F32).astype(BF16)
        out_slots[layer, pl.ds(zz * NY, NY)] = got.reshape(NY, slots, width)

    def send_all(layer, source):
        def plane(i, _):
            zz = lax.rem(z + order(i), NZ)
            select(layer, source, zz)
            for j in range(NY):
                slot_copy(layer, zz * NY + j).start()
            return 0

        lax.fori_loop(0, NZ - 1, plane, 0)
        select(layer, source, z)
        for j in range(1, NY):
            slot_copy(layer, z * NY + lax.rem(y + j, NY)).start()
        in_slots[layer, node] = out_slots[layer, node]

    def add_plane(layer, zz):
        ids = recv_live[zz]
        row_id = lax.broadcasted_iota(jnp.int32, (rows, slots), 0)
        for j in range(NY):
            place[:, j * slots:(j + 1) * slots] = jnp.where(
                row_id == ids[j:j + 1, :], 1.0, 0.0).astype(BF16)
        held = in_slots[layer, pl.ds(zz * NY, NY)].reshape(NY * slots, width)
        if layer == 0:
            held = jnp.concatenate([held, jnp.ones_like(held)], axis=1)
            both = jnp.dot(place[...], held, preferred_element_type=F32)
            total[...] += both[:, :width]
            degree[...] += both[:, width:]
        else:
            total[...] += jnp.dot(place[...], held, preferred_element_type=F32)

    def add_all(layer, middle=None):
        for j in range(1, NY):
            slot_wait(layer, z * NY + lax.rem(y + j, NY))
        add_plane(layer, z)

        def plane(i, _):
            zz = lax.rem(z + NZ - order(NZ - 2 - i), NZ)
            for j in range(NY):
                slot_wait(layer, zz * NY + j)
            add_plane(layer, zz)
            return 0

        if middle is None:
            lax.fori_loop(0, NZ - 1, plane, 0)
        else:
            lax.fori_loop(0, NZ - 3, plane, 0)
            middle()
            lax.fori_loop(NZ - 3, NZ - 1, plane, 0)

    def pass_w1():
        for dx in range(1, NX):
            w1_copy(dx).wait_recv()
            w1_pass(dx).start()

    for dx in range(1, NX):
        w1_copy(dx).start()
    w1_pass(0).start()

    send_all(0, x_ref)
    total[...] = x_ref[...].astype(F32)
    degree[...] = jnp.ones_like(degree)
    add_all(0, pass_w1)
    mine[...] = (total[...] / degree[...]).astype(BF16)

    def row_copy(step, d):
        other = lax.rem(feat + d, FEATS)
        if step == 0:
            source = mine.at[pl.ds(pl.multiple_of(other * part, 16), part)]
            target = rows_in.at[feat]
        else:
            source = rows_out.at[other]
            target = second.at[pl.ds(pl.multiple_of(feat * part, 16), part)]
        return pltpu.make_async_remote_copy(
            source, target, row_send.at[step, d], row_recv.at[step, d],
            device_id=(node, other), device_id_type=MESH)

    for d in range(1, FEATS):
        row_copy(0, d).start()
    rows_in[feat] = mine[pl.ds(pl.multiple_of(feat * part, 16), part)]
    for dx in range(NX):
        w1_pass(dx).wait_recv()
    w2_copy.wait()
    for d in range(1, FEATS):
        row_copy(0, d).wait_recv()

    held = jnp.concatenate([rows_in[f] for f in range(FEATS)], axis=1)
    hidden = jnp.dot(held, w1_all[...].reshape(FEATS * width, FEATS * width), preferred_element_type=F32)
    hidden = jnp.maximum(hidden, 0.0).astype(BF16)
    result = jnp.dot(hidden, w2_all[...], preferred_element_type=F32).astype(BF16)
    for f in range(FEATS):
        rows_out[f] = result[:, f * width:(f + 1) * width]
    for d in range(1, FEATS):
        row_copy(1, d).start()
    second[pl.ds(pl.multiple_of(feat * part, 16), part)] = rows_out[feat]
    for d in range(1, FEATS):
        row_copy(1, d).wait_recv()

    send_all(1, second)
    total[...] = second[...].astype(F32)
    add_all(1)
    out_ref[...] = (total[...] / degree[...]).astype(BF16)

    def sent(k, _):
        other = lax.rem(node + k, NODES)
        slot_copy(0, other).wait_send()
        slot_copy(1, other).wait_send()
        return 0

    lax.fori_loop(1, NODES, sent, 0)
    for dx in range(1, NX):
        w1_copy(dx).wait_send()
    for dx in range(NX):
        w1_pass(dx).wait_send()
    for d in range(1, FEATS):
        row_copy(0, d).wait_send()
        row_copy(1, d).wait_send()


def per_device(batch_node_input, weight_in, second_layer_weight, send_rows, recv_rows, block_count):
    rows, width = batch_node_input.shape
    nodes, slots = send_rows.shape[1:]
    part = rows // FEATS
    hidden = weight_in.shape[1]
    vmem = pl.BlockSpec(memory_space=pltpu.VMEM)
    dma = pltpu.SemaphoreType.DMA
    return pl.pallas_call(
        kernel,
        out_shape=jax.ShapeDtypeStruct((rows, width), BF16),
        in_specs=[vmem, vmem, pl.BlockSpec(memory_space=pl.ANY), vmem, vmem, vmem],
        out_specs=vmem,
        scratch_shapes=[
            pltpu.VMEM((FEATS, width, hidden), BF16),
            pltpu.VMEM((hidden, hidden), BF16),
            pltpu.VMEM((2, nodes, slots, width), BF16),
            pltpu.VMEM((2, nodes, slots, width), BF16),
            pltpu.VMEM((slots, nodes), F32),
            pltpu.VMEM((NZ, NY, slots), jnp.int32),
            pltpu.VMEM((NY * slots, rows), BF16),
            pltpu.VMEM((rows, NY * slots), BF16),
            pltpu.VMEM((rows, width), F32),
            pltpu.VMEM((rows, width), F32),
            pltpu.VMEM((rows, width), BF16),
            pltpu.VMEM((FEATS, part, width), BF16),
            pltpu.VMEM((FEATS, part, width), BF16),
            pltpu.VMEM((rows, width), BF16),
            dma((2, nodes)), dma((2, nodes)),
            dma((NX,)), dma((NX,)), dma((NX,)), dma((NX,)),
            dma((2, FEATS)), dma((2, FEATS)),
            dma,
        ],
        compiler_params=pltpu.CompilerParams(
            collective_id=0, has_side_effects=True, vmem_limit_bytes=48 * 2**20),
    )(batch_node_input, weight_in, second_layer_weight, send_rows[0], recv_rows[0], block_count[0])


def solution(mesh):
    return jax.shard_map(
        per_device, mesh=mesh,
        in_specs=(P("node", "feat"), P("feat", None), P(), P("node", None, None), P("node", None, None), P("node", None, None)),
        out_specs=P("node", "feat"), check_vma=False)
```

time: 204 us -> 96.4 us (0.47)
  the two profiles are of different devices: /device:TPU:32 before, /device:TPU:1 now
where the time goes in v1:
time: 96.4 us; the launch traced here: 96.1 us
  Pallas kernels  89.6 us (93%)
  local copies, waits for them, and re-layouts  6.45 us (7%)
    pallas_call x1, Pallas kernels, per_device(): pl.pallas_call(kernel, out_shape=jax.ShapeDtypeStruct((rows, width), BF16...  89.6 us
    unnamed x11, local copies, waits for them, and re-layouts  5.72 us

profile of v1, /device:TPU:1, one launch (start us, length us, event | category | flops | bytes accessed | tf_op | source)
XLA Modules:
  0.0 96.1 jit_solution(16485054746266780592)
XLA Ops:
  0.0 0.7 copy.7.count_ref
  0.7 0.0 copy-start
  0.7 1.6 %copy-done = bf16[1024,1024]{1,0:T(8,128)(2,1)S(1)} copy-done((bf16[1024,1024]{1,0:T(8,128)(2,1)S(1)}, bf16[1024,1024]{1,0:T(8,128)(2,1)}, u32[]{:S(2)}) %copy-start) | copy-done | bytes 2097176
  2.3 0.0 copy-start.1
  2.3 1.0 %copy-done.1 = bf16[1536,128]{1,0:T(8,128)(2,1)S(1)} copy-done((bf16[1536,128]{1,0:T(8,128)(2,1)S(1)}, bf16[1536,128]{1,0:T(8,128)(2,1)}, u32[]{:S(2)}) %copy-start.1) | copy-done | bytes 393240
  3.3 0.0 copy-start.2
  3.3 0.9 copy-done.2
  4.3 0.0 copy-start.3
  4.3 0.7 copy-done.3
  5.0 0.0 copy-start.4
  5.0 0.7 copy-done.4
  5.7 89.6 %shard_map.64 = bf16[1536,128]{1,0:T(8,128)(2,1)S(1)} custom-call(bf16[1536,128]{1,0:T(8,128)(2,1)S(1)} %copy-done.1, bf16[128,1024]{1,0:T(8,128)(2,1)S(1)} %copy-done.2, bf16[1024,1024]{1,0:T(8,128)(2,1)S(1)} %copy-done, s32[32,128]{1,0:T(8,128)S(1)} %bitcast.3, s32[32,128]{1,0:T(8,128)S(1)} %bitcast.4, s32[32,1]{1,0:T(8,128)S(1)} %copy.7.count_ref), custom_call_target="tpu_custom_call" | custom-call | tf_op jit(solution)/shard_map/pallas_call | solution.py:216
  95.3 0.7 copy.9
Async XLA Ops:
  0.7 1.6 %copy-start = (bf16[1024,1024]{1,0:T(8,128)(2,1)S(1)}, bf16[1024,1024]{1,0:T(8,128)(2,1)}, u32[]{:S(2)}) copy-start(bf16[1024,1024]{1,0:T(8,128)(2,1)} %w2_hbm.1) | copy-start | bytes 6291460
  2.3 1.0 %copy-start.1 = (bf16[1536,128]{1,0:T(8,128)(2,1)S(1)}, bf16[1536,128]{1,0:T(8,128)(2,1)}, u32[]{:S(2)}) copy-start(bf16[1536,128]{1,0:T(8,128)(2,1)} %x_ref.1) | copy-start | bytes 1179652
  3.3 0.9 copy-start.2
  4.3 0.7 copy-start.3
  5.0 0.7 copy-start.4

commit v2 on v1

--- a/solution.py
+++ b/solution.py
@@ -18,10 +18,10 @@
 
 
 def kernel(
-    x_ref, w1_ref, w2_hbm, send_ref, recv_ref, count_ref, out_ref,
-    w1_all, w2_all, out_slots, in_slots, send_cols, recv_live, pick, place,
+    x_hbm, w1_hbm, w2_hbm, send_hbm, recv_hbm, count_hbm, out_ref,
+    x_ref, send_ref, recv_ref, count_ref, w1_all, w2_all, out_slots, in_slots, send_cols, recv_live, pick, place,
     total, degree, mine, rows_in, rows_out, second,
-    slot_send, slot_recv, w1_send, w1_recv, w1_send2, w1_recv2, row_send, row_recv, w2_sem,
+    slot_send, slot_recv, w1_send, w1_recv, w1_send2, w1_recv2, row_send, row_recv, in_sem,
 ):
     rows, width = x_ref.shape
     slots = send_ref.shape[1]
@@ -32,39 +32,38 @@
 
     barrier = pltpu.get_barrier_semaphore()
 
-    def greet_node(k, _):
-        other = lax.rem(node + k, NODES)
-        pl.semaphore_signal(barrier, inc=1, device_id=(other, feat), device_id_type=MESH)
+    def greet_plane(i, _):
+        zz = lax.rem(z + order(i), NZ)
+        for j in range(NY):
+            pl.semaphore_signal(barrier, inc=1, device_id=(zz * NY + j, feat), device_id_type=MESH)
         return 0
 
-    def greet_feat(k, _):
-        other = lax.rem(feat + k, FEATS)
-        pl.semaphore_signal(barrier, inc=1, device_id=(node, other), device_id_type=MESH)
-        return 0
-
-    lax.fori_loop(1, FEATS, greet_feat, 0)
-    lax.fori_loop(1, NODES, greet_node, 0)
-
-    w2_copy = pltpu.make_async_copy(w2_hbm, w2_all, w2_sem)
-    w2_copy.start()
-    send_cols[...] = send_ref[...].astype(F32).T
-    slot_id = lax.broadcasted_iota(jnp.int32, recv_ref.shape, 1)
-    live = jnp.where(slot_id < count_ref[...], recv_ref[...], -1)
-    for q in range(NZ):
-        recv_live[q] = live[q * NY:(q + 1) * NY]
-    w1_all[feat] = w1_ref[...]
-
-    pl.semaphore_wait(barrier, NODES + FEATS - 2)
+    lax.fori_loop(0, NZ - 1, greet_plane, 0)
+    for j in range(1, NY):
+        pl.semaphore_signal(
+            barrier, inc=1, device_id=(z * NY + lax.rem(y + j, NY), feat), device_id_type=MESH)
+    for d in range(1, FEATS):
+        pl.semaphore_signal(
+            barrier, inc=1, device_id=(node, lax.rem(feat + d, FEATS)), device_id_type=MESH)
+
+    send_in = pltpu.make_async_copy(send_hbm, send_ref, in_sem.at[0])
+    x_in = pltpu.make_async_copy(x_hbm, x_ref, in_sem.at[1])
+    recv_in = pltpu.make_async_copy(recv_hbm, recv_ref, in_sem.at[2])
+    count_in = pltpu.make_async_copy(count_hbm, count_ref, in_sem.at[3])
+    w1_in = pltpu.make_async_copy(w1_hbm, w1_all.at[feat], in_sem.at[4])
+    w2_in = pltpu.make_async_copy(w2_hbm, w2_all, in_sem.at[5])
+    for copy in (send_in, x_in, recv_in, count_in, w1_in, w2_in):
+        copy.start()
 
     def w1_copy(dx):
         return pltpu.make_async_remote_copy(
-            w1_ref, w1_all.at[feat], w1_send.at[dx], w1_recv.at[dx],
+            w1_hbm, w1_all.at[feat], w1_send.at[dx], w1_recv.at[dx],
             device_id=(node, lax.rem(x + dx, NX) * NC + c), device_id_type=MESH)
 
     def w1_pass(dx):
         held = lax.rem(x + NX - dx, NX) * NC + c
         return pltpu.make_async_remote_copy(
-            w1_all.at[held], w1_all.at[held], w1_send2.at[dx], w1_recv2.at[dx],
+            w1_hbm if dx == 0 else w1_all.at[held], w1_all.at[held], w1_send2.at[dx], w1_recv2.at[dx],
             device_id=(node, x * NC + 1 - c), device_id_type=MESH)
 
     def slot_copy(layer, other):
@@ -79,44 +78,56 @@
             slot_send.at[layer, other], slot_recv.at[layer, other],
             device_id=(other, feat), device_id_type=MESH).wait_recv()
 
-    def select(layer, source, zz):
+    def build_pick(zz):
         cols = send_cols[...]
         lane = lax.broadcasted_iota(jnp.int32, cols.shape, 1)
         row_id = lax.broadcasted_iota(jnp.int32, (slots, rows), 1).astype(F32)
         for j in range(NY):
             col = jnp.sum(jnp.where(lane == zz * NY + j, cols, 0.0), axis=1, keepdims=True)
-            pick[j * slots:(j + 1) * slots, :] = jnp.where(row_id == col, 1.0, 0.0).astype(BF16)
-        got = jnp.dot(pick[...], source[...], preferred_element_type=F32).astype(BF16)
+            pick[zz, j * slots:(j + 1) * slots, :] = jnp.where(row_id == col, 1.0, 0.0).astype(BF16)
+
+    def select(layer, source, zz):
+        if layer == 0:
+            build_pick(zz)
+        got = jnp.dot(pick[zz], source[...], preferred_element_type=F32).astype(BF16)
         out_slots[layer, pl.ds(zz * NY, NY)] = got.reshape(NY, slots, width)
 
-    def send_all(layer, source):
+    def send_plane(layer, zz):
+        for j in range(NY):
+            slot_copy(layer, zz * NY + j).start()
+
+    def far(i):
+        return lax.rem(z + order(i), NZ)
+
+    def send_rest(layer, source, first):
         def plane(i, _):
-            zz = lax.rem(z + order(i), NZ)
-            select(layer, source, zz)
-            for j in range(NY):
-                slot_copy(layer, zz * NY + j).start()
+            select(layer, source, far(i))
+            send_plane(layer, far(i))
             return 0
 
-        lax.fori_loop(0, NZ - 1, plane, 0)
+        lax.fori_loop(first, NZ - 1, plane, 0)
         select(layer, source, z)
         for j in range(1, NY):
             slot_copy(layer, z * NY + lax.rem(y + j, NY)).start()
         in_slots[layer, node] = out_slots[layer, node]
 
-    def add_plane(layer, zz):
+    def build_place(zz, _):
         ids = recv_live[zz]
         row_id = lax.broadcasted_iota(jnp.int32, (rows, slots), 0)
         for j in range(NY):
-            place[:, j * slots:(j + 1) * slots] = jnp.where(
+            place[zz, :, j * slots:(j + 1) * slots] = jnp.where(
                 row_id == ids[j:j + 1, :], 1.0, 0.0).astype(BF16)
+        return 0
+
+    def add_plane(layer, zz):
         held = in_slots[layer, pl.ds(zz * NY, NY)].reshape(NY * slots, width)
         if layer == 0:
             held = jnp.concatenate([held, jnp.ones_like(held)], axis=1)
-            both = jnp.dot(place[...], held, preferred_element_type=F32)
+            both = jnp.dot(place[zz], held, preferred_element_type=F32)
             total[...] += both[:, :width]
             degree[...] += both[:, width:]
         else:
-            total[...] += jnp.dot(place[...], held, preferred_element_type=F32)
+            total[...] += jnp.dot(place[zz], held, preferred_element_type=F32)
 
     def add_all(layer, middle=None):
         for j in range(1, NY):
@@ -142,15 +153,40 @@
             w1_copy(dx).wait_recv()
             w1_pass(dx).start()
 
+    early = 2
+    send_in.wait()
+    send_cols[...] = send_ref[...].astype(F32).T
+    x_in.wait()
+    for i in range(early):
+        select(0, x_ref, far(i))
+
+    pl.semaphore_wait(barrier, NODES + FEATS - 2)
+
+    for i in range(early):
+        send_plane(0, far(i))
     for dx in range(1, NX):
         w1_copy(dx).start()
     w1_pass(0).start()
 
-    send_all(0, x_ref)
+    send_rest(0, x_ref, early)
+
+    recv_in.wait()
+    count_in.wait()
+    nodes = recv_ref.shape[0]
+    across = (lax.broadcasted_iota(jnp.int32, (nodes, nodes), 0)
+              == lax.broadcasted_iota(jnp.int32, (nodes, nodes), 1))
+    counts = jnp.sum(jnp.where(across, count_ref[...].astype(F32), 0.0), axis=1, keepdims=True)
+    slot_id = lax.broadcasted_iota(jnp.int32, recv_ref.shape, 1).astype(F32)
+    live = jnp.where(slot_id < counts, recv_ref[...], -1)
+    for q in range(NZ):
+        recv_live[q] = live[q * NY:(q + 1) * NY]
+    lax.fori_loop(0, NZ, build_place, 0)
+
     total[...] = x_ref[...].astype(F32)
     degree[...] = jnp.ones_like(degree)
     add_all(0, pass_w1)
-    mine[...] = (total[...] / degree[...]).astype(BF16)
+    degree[...] = 1.0 / degree[...]
+    mine[...] = (total[...] * degree[...]).astype(BF16)
 
     def row_copy(step, d):
         other = lax.rem(feat + d, FEATS)
@@ -169,7 +205,8 @@
     rows_in[feat] = mine[pl.ds(pl.multiple_of(feat * part, 16), part)]
     for dx in range(NX):
         w1_pass(dx).wait_recv()
-    w2_copy.wait()
+    w1_in.wait()
+    w2_in.wait()
     for d in range(1, FEATS):
         row_copy(0, d).wait_recv()
 
@@ -185,10 +222,10 @@
     for d in range(1, FEATS):
         row_copy(1, d).wait_recv()
 
-    send_all(1, second)
+    send_rest(1, second, 0)
     total[...] = second[...].astype(F32)
     add_all(1)
-    out_ref[...] = (total[...] / degree[...]).astype(BF16)
+    out_ref[...] = (total[...] * degree[...]).astype(BF16)
 
     def sent(k, _):
         other = lax.rem(node + k, NODES)
@@ -216,17 +253,21 @@
     return pl.pallas_call(
         kernel,
         out_shape=jax.ShapeDtypeStruct((rows, width), BF16),
-        in_specs=[vmem, vmem, pl.BlockSpec(memory_space=pl.ANY), vmem, vmem, vmem],
+        in_specs=[pl.BlockSpec(memory_space=pltpu.HBM)] * 6,
         out_specs=vmem,
         scratch_shapes=[
+            pltpu.VMEM((rows, width), BF16),
+            pltpu.VMEM((nodes, slots), jnp.int32),
+            pltpu.VMEM((nodes, slots), jnp.int32),
+            pltpu.VMEM((1, nodes), jnp.int32),
             pltpu.VMEM((FEATS, width, hidden), BF16),
             pltpu.VMEM((hidden, hidden), BF16),
             pltpu.VMEM((2, nodes, slots, width), BF16),
             pltpu.VMEM((2, nodes, slots, width), BF16),
             pltpu.VMEM((slots, nodes), F32),
             pltpu.VMEM((NZ, NY, slots), jnp.int32),
-            pltpu.VMEM((NY * slots, rows), BF16),
-            pltpu.VMEM((rows, NY * slots), BF16),
+            pltpu.VMEM((NZ, NY * slots, rows), BF16),
+            pltpu.VMEM((NZ, rows, NY * slots), BF16),
             pltpu.VMEM((rows, width), F32),
             pltpu.VMEM((rows, width), F32),
             pltpu.VMEM((rows, width), BF16),
@@ -236,11 +277,11 @@
             dma((2, nodes)), dma((2, nodes)),
             dma((NX,)), dma((NX,)), dma((NX,)), dma((NX,)),
             dma((2, FEATS)), dma((2, FEATS)),
-            dma,
+            dma((6,)),
         ],
         compiler_params=pltpu.CompilerParams(
-            collective_id=0, has_side_effects=True, vmem_limit_bytes=48 * 2**20),
-    )(batch_node_input, weight_in, second_layer_weight, send_rows[0], recv_rows[0], block_count[0])
+            collective_id=0, has_side_effects=True, vmem_limit_bytes=60 * 2**20),
+    )(batch_node_input, weight_in, second_layer_weight, send_rows[0], recv_rows[0], block_count[:, :, 0])
 
 
 def solution(mesh):

time: 96.4 us -> 89.7 us (0.930)
  local copies, waits for them, and re-layouts: 6.45 us -> 1.77 us
  Pallas kernels: 89.6 us -> 87.8 us
    unnamed x11 -> x1, local copies, waits for them, and re-layouts: 5.72 us -> 1.77 us
    pallas_call x1, Pallas kernels: 89.6 us -> 87.8 us  [per_device(): pl.pallas_call(kernel, out_shape=jax.ShapeDtypeStruct((rows, width), BF16...]
where the time goes in v2:
time: 89.7 us; the launch traced here: 89.6 us
  Pallas kernels  87.8 us (98%)
  local copies, waits for them, and re-layouts  1.77 us (2%)
    pallas_call x1, Pallas kernels, per_device(): pl.pallas_call(kernel, out_shape=jax.ShapeDtypeStruct((rows, width), BF16...  87.8 us

profile of v2, /device:TPU:1, one launch (start us, length us, event | category | flops | bytes accessed | tf_op | source)
XLA Modules:
  0.0 89.6 jit_solution(5636785534621558744)
XLA Ops:
  0.0 87.8 %shard_map.64 = bf16[1536,128]{1,0:T(8,128)(2,1)} custom-call(bf16[1536,128]{1,0:T(8,128)(2,1)} %x_hbm.1, bf16[128,1024]{1,0:T(8,128)(2,1)} %w1_hbm.1, bf16[1024,1024]{1,0:T(8,128)(2,1)} %w2_hbm.1, s32[32,128]{1,0:T(8,128)} %bitcast.3, s32[32,128]{1,0:T(8,128)} %bitcast.4, s32[1,32]{1,0:T(1,128)} %bitcast.5), custom_call_target="tpu_custom_call" | custom-call | tf_op jit(solution)/shard_map/pallas_call | solution.py:253
  87.8 1.8 %copy.8 = bf16[1536,128]{1,0:T(8,128)(2,1)} copy(bf16[1536,128]{1,0:T(8,128)(2,1)} %shard_map.64) | data formatting | bytes 786432

commit v3 on v2

--- a/solution.py
+++ b/solution.py
@@ -96,13 +96,13 @@
         for j in range(NY):
             slot_copy(layer, zz * NY + j).start()
 
-    def far(i):
-        return lax.rem(z + order(i), NZ)
+    def near(i):
+        return lax.rem(z + order(NZ - 2 - i), NZ)
 
     def send_rest(layer, source, first):
         def plane(i, _):
-            select(layer, source, far(i))
-            send_plane(layer, far(i))
+            select(layer, source, near(i))
+            send_plane(layer, near(i))
             return 0
 
         lax.fori_loop(first, NZ - 1, plane, 0)
@@ -158,12 +158,12 @@
     send_cols[...] = send_ref[...].astype(F32).T
     x_in.wait()
     for i in range(early):
-        select(0, x_ref, far(i))
+        select(0, x_ref, near(i))
 
     pl.semaphore_wait(barrier, NODES + FEATS - 2)
 
     for i in range(early):
-        send_plane(0, far(i))
+        send_plane(0, near(i))
     for dx in range(1, NX):
         w1_copy(dx).start()
     w1_pass(0).start()
@@ -280,7 +280,7 @@
             dma((6,)),
         ],
         compiler_params=pltpu.CompilerParams(
-            collective_id=0, has_side_effects=True, vmem_limit_bytes=60 * 2**20),
+            collective_id=0, has_side_effects=True, vmem_limit_bytes=44 * 2**20),
     )(batch_node_input, weight_in, second_layer_weight, send_rows[0], recv_rows[0], block_count[:, :, 0])
 
 

time: 89.7 us -> 85.9 us (0.958)
  the two profiles are of different devices: /device:TPU:1 before, /device:TPU:32 now
where the time goes in v3:
time: 85.9 us; the launch traced here: 84.6 us
  Pallas kernels  78.2 us (91%)
  local copies, waits for them, and re-layouts  6.37 us (7%)
    pallas_call x1, Pallas kernels, per_device(): pl.pallas_call(kernel, out_shape=jax.ShapeDtypeStruct((rows, width), BF16...  78.2 us
    unnamed x13, local copies, waits for them, and re-layouts  6.37 us

profile of v3, /device:TPU:32, one launch (start us, length us, event | category | flops | bytes accessed | tf_op | source)
XLA Modules:
  0.0 84.6 jit_solution(16654763711509070541)
XLA Ops:
  0.0 0.0 copy-start
  0.0 1.6 %copy-done = bf16[1024,1024]{1,0:T(8,128)(2,1)S(1)} copy-done((bf16[1024,1024]{1,0:T(8,128)(2,1)S(1)}, bf16[1024,1024]{1,0:T(8,128)(2,1)}, u32[]{:S(2)}) %copy-start) | copy-done | bytes 2097176
  1.6 0.0 copy-start.1
  1.6 1.0 %copy-done.1 = bf16[1536,128]{1,0:T(8,128)(2,1)S(1)} copy-done((bf16[1536,128]{1,0:T(8,128)(2,1)S(1)}, bf16[1536,128]{1,0:T(8,128)(2,1)}, u32[]{:S(2)}) %copy-start.1) | copy-done | bytes 393240
  2.6 0.0 copy-start.2
  2.6 0.9 %copy-done.2 = bf16[128,1024]{1,0:T(8,128)(2,1)S(1)} copy-done((bf16[128,1024]{1,0:T(8,128)(2,1)S(1)}, bf16[128,1024]{1,0:T(8,128)(2,1)}, u32[]{:S(2)}) %copy-start.2) | copy-done | bytes 262168
  3.5 0.0 copy-start.3
  3.5 0.7 copy-done.3
  4.3 0.0 copy-start.4
  4.3 0.7 copy-done.4
  5.0 0.0 copy-start.5
  5.0 0.7 copy-done.5
  5.6 78.2 %shard_map.64 = bf16[1536,128]{1,0:T(8,128)(2,1)S(1)} custom-call(bf16[1536,128]{1,0:T(8,128)(2,1)S(1)} %copy-done.1, bf16[128,1024]{1,0:T(8,128)(2,1)S(1)} %copy-done.2, bf16[1024,1024]{1,0:T(8,128)(2,1)S(1)} %copy-done, s32[32,128]{1,0:T(8,128)S(1)} %bitcast.3, s32[32,128]{1,0:T(8,128)S(1)} %bitcast.4, s32[1,32]{1,0:T(1,128)S(1)} %bitcast.5), custom_call_target="tpu_custom_call" | custom-call | tf_op jit(solution)/shard_map/pallas_call | solution.py:253
  83.8 0.7 copy.8
Async XLA Ops:
  0.0 1.6 %copy-start = (bf16[1024,1024]{1,0:T(8,128)(2,1)S(1)}, bf16[1024,1024]{1,0:T(8,128)(2,1)}, u32[]{:S(2)}) copy-start(bf16[1024,1024]{1,0:T(8,128)(2,1)} %w2_hbm.1) | copy-start | bytes 6291460
  1.6 1.0 %copy-start.1 = (bf16[1536,128]{1,0:T(8,128)(2,1)S(1)}, bf16[1536,128]{1,0:T(8,128)(2,1)}, u32[]{:S(2)}) copy-start(bf16[1536,128]{1,0:T(8,128)(2,1)} %x_hbm.1) | copy-start | bytes 1179652
  2.6 0.9 %copy-start.2 = (bf16[128,1024]{1,0:T(8,128)(2,1)S(1)}, bf16[128,1024]{1,0:T(8,128)(2,1)}, u32[]{:S(2)}) copy-start(bf16[128,1024]{1,0:T(8,128)(2,1)} %w1_hbm.1) | copy-start | bytes 786436
  3.5 0.7 copy-start.3
  4.3 0.7 copy-start.4
  5.0 0.7 copy-start.5

commit v4 on v3

--- a/solution.py
+++ b/solution.py
@@ -10,6 +10,8 @@
 MESH = pl.DeviceIdType.MESH
 NZ, NY, NX, NC = 8, 4, 4, 2
 NODES, FEATS = NZ * NY, NX * NC
+PIECES = 2
+FEAT_STEPS = ((2, 0), (2, 1), (1, 0), (3, 0), (1, 1), (3, 1), (0, 1))
 BF16, F32 = jnp.bfloat16, jnp.float32
 
 
@@ -117,17 +119,13 @@
         for j in range(NY):
             place[zz, :, j * slots:(j + 1) * slots] = jnp.where(
                 row_id == ids[j:j + 1, :], 1.0, 0.0).astype(BF16)
+        degree[...] += jnp.dot(
+            place[zz], jnp.ones((NY * slots, width), BF16), preferred_element_type=F32)
         return 0
 
     def add_plane(layer, zz):
         held = in_slots[layer, pl.ds(zz * NY, NY)].reshape(NY * slots, width)
-        if layer == 0:
-            held = jnp.concatenate([held, jnp.ones_like(held)], axis=1)
-            both = jnp.dot(place[zz], held, preferred_element_type=F32)
-            total[...] += both[:, :width]
-            degree[...] += both[:, width:]
-        else:
-            total[...] += jnp.dot(place[zz], held, preferred_element_type=F32)
+        total[...] += jnp.dot(place[zz], held, preferred_element_type=F32)
 
     def add_all(layer, middle=None):
         for j in range(1, NY):
@@ -180,47 +178,54 @@
     live = jnp.where(slot_id < counts, recv_ref[...], -1)
     for q in range(NZ):
         recv_live[q] = live[q * NY:(q + 1) * NY]
+    degree[...] = jnp.ones_like(degree)
     lax.fori_loop(0, NZ, build_place, 0)
+    degree[...] = 1.0 / degree[...]
 
     total[...] = x_ref[...].astype(F32)
-    degree[...] = jnp.ones_like(degree)
     add_all(0, pass_w1)
-    degree[...] = 1.0 / degree[...]
     mine[...] = (total[...] * degree[...]).astype(BF16)
 
-    def row_copy(step, d):
-        other = lax.rem(feat + d, FEATS)
+    piece = part // PIECES
+
+    def row_copy(step, h, d):
+        dx, dc = FEAT_STEPS[d]
+        other = lax.rem(x + dx, NX) * NC + lax.rem(c + dc, NC)
         if step == 0:
-            source = mine.at[pl.ds(pl.multiple_of(other * part, 16), part)]
-            target = rows_in.at[feat]
+            source = mine.at[pl.ds(pl.multiple_of(other * part + h * piece, 16), piece)]
+            target = rows_in.at[feat, pl.ds(h * piece, piece)]
         else:
-            source = rows_out.at[other]
-            target = second.at[pl.ds(pl.multiple_of(feat * part, 16), part)]
-        return pltpu.make_async_remote_copy(
-            source, target, row_send.at[step, d], row_recv.at[step, d],
+            source = rows_out.at[other, pl.ds(h * piece, piece)]
+            target = second.at[pl.ds(pl.multiple_of(feat * part + h * piece, 16), piece)]
+        return pltpu.make_async_remote_copy(
+            source, target, row_send.at[step, h, d], row_recv.at[step, h, d],
             device_id=(node, other), device_id_type=MESH)
 
-    for d in range(1, FEATS):
-        row_copy(0, d).start()
+    each = range(len(FEAT_STEPS))
+    for h in range(PIECES):
+        for d in each:
+            row_copy(0, h, d).start()
     rows_in[feat] = mine[pl.ds(pl.multiple_of(feat * part, 16), part)]
     for dx in range(NX):
         w1_pass(dx).wait_recv()
     w1_in.wait()
     w2_in.wait()
-    for d in range(1, FEATS):
-        row_copy(0, d).wait_recv()
-
-    held = jnp.concatenate([rows_in[f] for f in range(FEATS)], axis=1)
-    hidden = jnp.dot(held, w1_all[...].reshape(FEATS * width, FEATS * width), preferred_element_type=F32)
-    hidden = jnp.maximum(hidden, 0.0).astype(BF16)
-    result = jnp.dot(hidden, w2_all[...], preferred_element_type=F32).astype(BF16)
-    for f in range(FEATS):
-        rows_out[f] = result[:, f * width:(f + 1) * width]
-    for d in range(1, FEATS):
-        row_copy(1, d).start()
+    for h in range(PIECES):
+        for d in each:
+            row_copy(0, h, d).wait_recv()
+        held = jnp.concatenate([rows_in[f, h * piece:(h + 1) * piece] for f in range(FEATS)], axis=1)
+        hidden = jnp.dot(
+            held, w1_all[...].reshape(FEATS * width, FEATS * width), preferred_element_type=F32)
+        hidden = jnp.maximum(hidden, 0.0).astype(BF16)
+        result = jnp.dot(hidden, w2_all[...], preferred_element_type=F32).astype(BF16)
+        for f in range(FEATS):
+            rows_out[f, h * piece:(h + 1) * piece] = result[:, f * width:(f + 1) * width]
+        for d in each:
+            row_copy(1, h, d).start()
     second[pl.ds(pl.multiple_of(feat * part, 16), part)] = rows_out[feat]
-    for d in range(1, FEATS):
-        row_copy(1, d).wait_recv()
+    for h in range(PIECES):
+        for d in each:
+            row_copy(1, h, d).wait_recv()
 
     send_rest(1, second, 0)
     total[...] = second[...].astype(F32)
@@ -238,9 +243,10 @@
         w1_copy(dx).wait_send()
     for dx in range(NX):
         w1_pass(dx).wait_send()
-    for d in range(1, FEATS):
-        row_copy(0, d).wait_send()
-        row_copy(1, d).wait_send()
+    for h in range(PIECES):
+        for d in each:
+            row_copy(0, h, d).wait_send()
+            row_copy(1, h, d).wait_send()
 
 
 def per_device(batch_node_input, weight_in, second_layer_weight, send_rows, recv_rows, block_count):
@@ -276,11 +282,11 @@
             pltpu.VMEM((rows, width), BF16),
             dma((2, nodes)), dma((2, nodes)),
             dma((NX,)), dma((NX,)), dma((NX,)), dma((NX,)),
-            dma((2, FEATS)), dma((2, FEATS)),
+            dma((2, PIECES, FEATS)), dma((2, PIECES, FEATS)),
             dma((6,)),
         ],
         compiler_params=pltpu.CompilerParams(
-            collective_id=0, has_side_effects=True, vmem_limit_bytes=44 * 2**20),
+            collective_id=0, has_side_effects=True, vmem_limit_bytes=60 * 2**20),
     )(batch_node_input, weight_in, second_layer_weight, send_rows[0], recv_rows[0], block_count[:, :, 0])
 
 

time: 85.9 us -> 81 us (0.943)
  the two profiles are of different devices: /device:TPU:32 before, /device:TPU:40 now
where the time goes in v4:
time: 81 us; the launch traced here: 80.8 us
  Pallas kernels  79.1 us (98%)
  local copies, waits for them, and re-layouts  1.77 us (2%)
    pallas_call x1, Pallas kernels, per_device(): pl.pallas_call(kernel, out_shape=jax.ShapeDtypeStruct((rows, width), BF16...  79.1 us
    unnamed x1, local copies, waits for them, and re-layouts  1.77 us

profile of v4, /device:TPU:40, one launch (start us, length us, event | category | flops | bytes accessed | tf_op | source)
XLA Modules:
  0.0 80.8 jit_solution(8409559418718220514)
XLA Ops:
  0.0 79.1 %shard_map.64 = bf16[1536,128]{1,0:T(8,128)(2,1)} custom-call(bf16[1536,128]{1,0:T(8,128)(2,1)} %x_hbm.1, bf16[128,1024]{1,0:T(8,128)(2,1)} %w1_hbm.1, bf16[1024,1024]{1,0:T(8,128)(2,1)} %w2_hbm.1, s32[32,128]{1,0:T(8,128)} %bitcast.3, s32[32,128]{1,0:T(8,128)} %bitcast.4, s32[1,32]{1,0:T(1,128)} %bitcast.5), custom_call_target="tpu_custom_call" | custom-call | tf_op jit(solution)/shard_map/pallas_call | solution.py:259
  79.1 1.8 %copy.8 = bf16[1536,128]{1,0:T(8,128)(2,1)} copy(bf16[1536,128]{1,0:T(8,128)(2,1)} %shard_map.64) | data formatting | bytes 786432

commit v5 on v4

--- a/solution.py
+++ b/solution.py
@@ -11,6 +11,8 @@
 NZ, NY, NX, NC = 8, 4, 4, 2
 NODES, FEATS = NZ * NY, NX * NC
 PIECES = 2
+BASE = 64
+CAPS = (352, 304, 224, 128)
 FEAT_STEPS = ((2, 0), (2, 1), (1, 0), (3, 0), (1, 1), (3, 1), (0, 1))
 BF16, F32 = jnp.bfloat16, jnp.float32
 
@@ -19,11 +21,24 @@
     return lax.rem(4 + lax.rem(i, 2) * ((i + 1) // 2) - (1 - lax.rem(i, 2)) * (i // 2), NZ)
 
 
-def kernel(
-    x_hbm, w1_hbm, w2_hbm, send_hbm, recv_hbm, count_hbm, out_ref,
+def kernel(packed, x_hbm, w1_hbm, w2_hbm, send_hbm, recv_hbm, count_hbm, out_ref, *refs):
+    if packed:
+        over_ref, *refs = refs
+        (count_all, count_mat, spots, pack, unpack1, unpack2, unpack3, unpack4, parcel, hop1, hop2, hop3, hop4, handed,
+         count_send, count_recv, hop_send, hop_recv, hand_send, hand_recv) = refs[27:]
+        unpacks, hops = (unpack1, unpack2, unpack3, unpack4), (hop1, hop2, hop3, hop4)
+    run(packed, x_hbm, w1_hbm, w2_hbm, send_hbm, recv_hbm, count_hbm, out_ref,
+        *(refs[:27]), *((over_ref, count_all, count_mat, spots, pack, unpacks, parcel, hops, handed,
+                         count_send, count_recv, hop_send, hop_recv, hand_send, hand_recv) if packed else (None,) * 15))
+
+
+def run(
+    packed, x_hbm, w1_hbm, w2_hbm, send_hbm, recv_hbm, count_hbm, out_ref,
     x_ref, send_ref, recv_ref, count_ref, w1_all, w2_all, out_slots, in_slots, send_cols, recv_live, pick, place,
     total, degree, mine, rows_in, rows_out, second,
     slot_send, slot_recv, w1_send, w1_recv, w1_send2, w1_recv2, row_send, row_recv, in_sem,
+    over_ref, count_all, count_mat, spots, pack, unpacks, parcel, hops, handed,
+    count_send, count_recv, hop_send, hop_recv, hand_send, hand_recv,
 ):
     rows, width = x_ref.shape
     slots = send_ref.shape[1]
@@ -68,15 +83,18 @@
             w1_hbm if dx == 0 else w1_all.at[held], w1_all.at[held], w1_send2.at[dx], w1_recv2.at[dx],
             device_id=(node, x * NC + 1 - c), device_id_type=MESH)
 
-    def slot_copy(layer, other):
-        return pltpu.make_async_remote_copy(
-            out_slots.at[layer, other], in_slots.at[layer, node],
+    base = BASE if packed else slots
+    rest = slots - base
+
+    def slot_copy(layer, other, count):
+        return pltpu.make_async_remote_copy(
+            out_slots.at[layer, other, pl.ds(0, count)], in_slots.at[layer, node, pl.ds(0, count)],
             slot_send.at[layer, other], slot_recv.at[layer, node],
             device_id=(other, feat), device_id_type=MESH)
 
-    def slot_wait(layer, other):
+    def slot_wait(layer, other, count):
         pltpu.make_async_remote_copy(
-            out_slots.at[layer, other], in_slots.at[layer, other],
+            out_slots.at[layer, other, pl.ds(0, count)], in_slots.at[layer, other, pl.ds(0, count)],
             slot_send.at[layer, other], slot_recv.at[layer, other],
             device_id=(other, feat), device_id_type=MESH).wait_recv()
 
@@ -94,9 +112,9 @@
         got = jnp.dot(pick[zz], source[...], preferred_element_type=F32).astype(BF16)
         out_slots[layer, pl.ds(zz * NY, NY)] = got.reshape(NY, slots, width)
 
-    def send_plane(layer, zz):
-        for j in range(NY):
-            slot_copy(layer, zz * NY + j).start()
+    def send_plane(layer, zz, ys=range(NY)):
+        for j in ys:
+            slot_copy(layer, zz * NY + j, base).start()
 
     def near(i):
         return lax.rem(z + order(NZ - 2 - i), NZ)
@@ -107,10 +125,10 @@
             send_plane(layer, near(i))
             return 0
 
-        lax.fori_loop(first, NZ - 1, plane, 0)
+        lax.fori_loop(first, 4 if packed else NZ - 1, plane, 0)
         select(layer, source, z)
         for j in range(1, NY):
-            slot_copy(layer, z * NY + lax.rem(y + j, NY)).start()
+            slot_copy(layer, z * NY + lax.rem(y + j, NY), slots).start()
         in_slots[layer, node] = out_slots[layer, node]
 
     def build_place(zz, _):
@@ -119,32 +137,193 @@
         for j in range(NY):
             place[zz, :, j * slots:(j + 1) * slots] = jnp.where(
                 row_id == ids[j:j + 1, :], 1.0, 0.0).astype(BF16)
-        degree[...] += jnp.dot(
-            place[zz], jnp.ones((NY * slots, width), BF16), preferred_element_type=F32)
         return 0
 
     def add_plane(layer, zz):
         held = in_slots[layer, pl.ds(zz * NY, NY)].reshape(NY * slots, width)
-        total[...] += jnp.dot(place[zz], held, preferred_element_type=F32)
-
-    def add_all(layer, middle=None):
+        if layer == 0:
+            held = jnp.concatenate([held, jnp.ones_like(held)], axis=1)
+            both = jnp.dot(place[zz], held, preferred_element_type=F32)
+            total[...] += both[:, :width]
+            degree[...] += both[:, width:]
+        else:
+            total[...] += jnp.dot(place[zz], held, preferred_element_type=F32)
+
+    def add_near(layer):
         for j in range(1, NY):
-            slot_wait(layer, z * NY + lax.rem(y + j, NY))
+            slot_wait(layer, z * NY + lax.rem(y + j, NY), slots)
         add_plane(layer, z)
 
+    def add_far(layer, first, last):
         def plane(i, _):
             zz = lax.rem(z + NZ - order(NZ - 2 - i), NZ)
             for j in range(NY):
-                slot_wait(layer, zz * NY + j)
+                slot_wait(layer, zz * NY + j, base)
+            if packed:
+                for j in range(1, NY):
+                    hand_wait(layer, zz * NY + lax.rem(y + j, NY))
             add_plane(layer, zz)
             return 0
 
-        if middle is None:
-            lax.fori_loop(0, NZ - 1, plane, 0)
-        else:
-            lax.fori_loop(0, NZ - 3, plane, 0)
+        lax.fori_loop(first, last, plane, 0)
+
+    def count_copy(other):
+        return pltpu.make_async_remote_copy(
+            count_ref, count_all.at[node], count_send.at[other], count_recv.at[node],
+            device_id=(other, feat), device_id_type=MESH)
+
+    def count_wait(other):
+        pltpu.make_async_remote_copy(
+            count_ref, count_all.at[other], count_send.at[other], count_recv.at[other],
+            device_id=(other, feat), device_id_type=MESH).wait_recv()
+
+    def hop_copy(layer, way, h):
+        source = parcel.at[layer, way] if h == 0 else hops[h - 1].at[layer, way, pl.ds(0, CAPS[h])]
+        return pltpu.make_async_remote_copy(
+            source, hops[h].at[layer, way], hop_send.at[layer, way, h], hop_recv.at[layer, way, h],
+            device_id=(lax.rem(z + (1 if way == 0 else NZ - 1), NZ) * NY + y, feat), device_id_type=MESH)
+
+    def origin(way, h):
+        return lax.rem(z + (NZ - 1 - h if way == 0 else h + 1), NZ) * NY + y
+
+    def hand_copy(layer, way, h, j):
+        return pltpu.make_async_remote_copy(
+            handed.at[layer, way, h, j], in_slots.at[layer, origin(way, h), pl.ds(base, rest)],
+            hand_send.at[layer, way, h, j], hand_recv.at[layer, origin(way, h)],
+            device_id=(z * NY + j, feat), device_id_type=MESH)
+
+    def hand_wait(layer, other):
+        pltpu.make_async_remote_copy(
+            handed.at[layer, 0, 0, 0], in_slots.at[layer, other, pl.ds(base, rest)],
+            hand_send.at[layer, 0, 0, 0], hand_recv.at[layer, other],
+            device_id=(other, feat), device_id_type=MESH).wait_recv()
+
+    def ends(way, h):
+        return range(NY) if h < 3 else range(0, 2) if way == 0 else range(2, NY)
+
+    def way_and_steps(there, here):
+        step = (there // NY + NZ - here) & (NZ - 1)
+        low = (there & (NY - 1)) < 2
+        up = ((step >= 1) & (step <= 3)) | ((step == 4) & low)
+        away = jnp.where(step <= 4, step, NZ - step)
+        return jnp.where(step == 0, 2, jnp.where(up, 0, 1)), away
+
+    def plan(source, ov, ov_t):
+        here = source // NY
+        square = (NODES, NODES)
+        sub = lax.broadcasted_iota(jnp.int32, square, 0)
+        lane = lax.broadcasted_iota(jnp.int32, square, 1)
+        row = jnp.sum(jnp.where(sub == source, ov_t, 0.0), axis=0, keepdims=True)
+        col = jnp.sum(jnp.where(lane == source, ov, 0.0), axis=1, keepdims=True)
+        way, away = way_and_steps(sub, here)
+        way_l, away_l = way_and_steps(lane, here)
+        before = (way == way_l) & ((away_l > away) | ((away_l == away) & ((lane & (NY - 1)) < (sub & (NY - 1)))))
+        offset = jnp.sum(jnp.where(before, row, 0.0), axis=1, keepdims=True)
+        slot = lax.broadcasted_iota(jnp.int32, (NODES, slots), 1).astype(F32) - float(base)
+        return jnp.where((slot >= 0.0) & (slot < col), offset + slot, -1.0)
+
+    def prepare():
+        lax.fori_loop(1, NODES, lambda k, _: (count_wait(lax.rem(node + k, NODES)), 0)[1], 0)
+        count_mat[...] = jnp.zeros_like(count_mat)
+        for p in range(NODES):
+            count_mat[p:p + 1, :NODES] = count_all[p].astype(F32)
+        ov_wide = jnp.maximum(count_mat[...] - float(base), 0.0)
+        ov = ov_wide[:, :NODES]
+        ov_t = ov_wide.T[:NODES, :]
+        square = (NODES, NODES)
+        sub = lax.broadcasted_iota(jnp.int32, square, 0)
+        lane = lax.broadcasted_iota(jnp.int32, square, 1)
+        way, away = way_and_steps(lane, sub // NY)
+        worst = jnp.zeros((NODES, 1), F32)
+        for w in range(2):
+            for h in range(4):
+                load = jnp.sum(jnp.where((way == w) & (away > h), ov_t, 0.0), axis=1, keepdims=True)
+                worst = jnp.maximum(worst, load - float(CAPS[h]))
+        over_ref[...] = jnp.zeros(over_ref.shape, F32) + jnp.max(worst, axis=0, keepdims=True)
+        mine_spots = plan(node, ov, ov_t)
+        for q in range(NZ):
+            spots[q] = mine_spots[q * NY:(q + 1) * NY]
+        for w in range(2):
+            for h in range(4):
+                ids = spots[lax.rem(z + (h + 1 if w == 0 else NZ - 1 - h), NZ)]
+                row_id = lax.broadcasted_iota(jnp.int32, (CAPS[0], slots), 0).astype(F32)
+                for j in ends(w, h):
+                    pack[w, h, :, j * slots:(j + 1) * slots] = jnp.where(
+                        row_id == ids[j:j + 1, :], 1.0, 0.0).astype(BF16)
+        return ov, ov_t
+
+    def prepare_unpack(ov, ov_t):
+        for w in range(2):
+            for h in range(4):
+                columns = plan(origin(w, h), ov, ov_t).T
+                lane = lax.broadcasted_iota(jnp.int32, columns.shape, 1)
+                row_id = lax.broadcasted_iota(jnp.int32, (rest, CAPS[h]), 1).astype(F32)
+                for j in ends(w, h):
+                    col = jnp.sum(jnp.where(lane == z * NY + j, columns, 0.0), axis=1, keepdims=True)
+                    unpacks[h][w, j * rest:(j + 1) * rest, :] = jnp.where(
+                        row_id == col[base:, :], 1.0, 0.0).astype(BF16)
+
+    def start_hops(layer):
+        for w in range(2):
+            got = jnp.zeros((CAPS[0], width), F32)
+            for h in range(4):
+                zz = lax.rem(z + (h + 1 if w == 0 else NZ - 1 - h), NZ)
+                first, last = ends(w, h)[0], ends(w, h)[-1] + 1
+                held = out_slots[layer, pl.ds(zz * NY + first, last - first)].reshape((last - first) * slots, width)
+                got += jnp.dot(pack[w, h, :, first * slots:last * slots], held, preferred_element_type=F32)
+            parcel[layer, w] = got.astype(BF16)
+            hop_copy(layer, w, 0).start()
+
+    def take_hop(layer, h):
+        for w in range(2):
+            hop_copy(layer, w, h).wait_recv()
+            if h < 3:
+                hop_copy(layer, w, h + 1).start()
+        for w in range(2):
+            first, last = ends(w, h)[0], ends(w, h)[-1] + 1
+            got = jnp.dot(
+                unpacks[h][w, first * rest:last * rest, :], hops[h][layer, w], preferred_element_type=F32).astype(BF16)
+            for j in ends(w, h):
+                handed[layer, w, h, j] = got[(j - first) * rest:(j - first + 1) * rest]
+
+                @pl.when(y != j)
+                def _():
+                    hand_copy(layer, w, h, j).start()
+
+                @pl.when(y == j)
+                def _():
+                    in_slots[layer, origin(w, h), base:] = got[(j - first) * rest:(j - first + 1) * rest]
+
+    def sent_hops(layer):
+        for w in range(2):
+            for h in range(4):
+                hop_copy(layer, w, h).wait_send()
+                for j in ends(w, h):
+                    @pl.when(y != j)
+                    def _():
+                        hand_copy(layer, w, h, j).wait_send()
+
+    def select_last(layer, source):
+        lax.fori_loop(4, NZ - 1, lambda i, _: (select(layer, source, near(i)), 0)[1], 0)
+
+    def finish_packed(layer, middle=None):
+        for zz in (near(4), near(5)):
+            send_plane(layer, zz, (0, 1))
+        if middle is not None:
             middle()
-            lax.fori_loop(NZ - 3, NZ - 1, plane, 0)
+        add_near(layer)
+        take_hop(layer, 0)
+        for zz in (near(4), near(5)):
+            send_plane(layer, zz, (2, 3))
+        take_hop(layer, 1)
+        send_plane(layer, near(6))
+        add_far(layer, 0, 2)
+        take_hop(layer, 2)
+        add_far(layer, 2, 4)
+        take_hop(layer, 3)
+        if layer == 0:
+            pass_w1()
+        add_far(layer, 4, 7)
 
     def pass_w1():
         for dx in range(1, NX):
@@ -152,6 +331,7 @@
             w1_pass(dx).start()
 
     early = 2
+    count_in.wait()
     send_in.wait()
     send_cols[...] = send_ref[...].astype(F32).T
     x_in.wait()
@@ -160,6 +340,16 @@
 
     pl.semaphore_wait(barrier, NODES + FEATS - 2)
 
+    if packed:
+        def tell(i, _):
+            for j in range(NY):
+                count_copy(lax.rem(z + order(i), NZ) * NY + j).start()
+            return 0
+
+        lax.fori_loop(0, NZ - 1, tell, 0)
+        for j in range(1, NY):
+            count_copy(z * NY + lax.rem(y + j, NY)).start()
+        count_all[node] = count_ref[...]
     for i in range(early):
         send_plane(0, near(i))
     for dx in range(1, NX):
@@ -168,22 +358,37 @@
 
     send_rest(0, x_ref, early)
 
-    recv_in.wait()
-    count_in.wait()
-    nodes = recv_ref.shape[0]
-    across = (lax.broadcasted_iota(jnp.int32, (nodes, nodes), 0)
-              == lax.broadcasted_iota(jnp.int32, (nodes, nodes), 1))
-    counts = jnp.sum(jnp.where(across, count_ref[...].astype(F32), 0.0), axis=1, keepdims=True)
-    slot_id = lax.broadcasted_iota(jnp.int32, recv_ref.shape, 1).astype(F32)
-    live = jnp.where(slot_id < counts, recv_ref[...], -1)
-    for q in range(NZ):
-        recv_live[q] = live[q * NY:(q + 1) * NY]
-    degree[...] = jnp.ones_like(degree)
-    lax.fori_loop(0, NZ, build_place, 0)
+    def prepare_place():
+        recv_in.wait()
+        nodes = recv_ref.shape[0]
+        across = (lax.broadcasted_iota(jnp.int32, (nodes, nodes), 0)
+                  == lax.broadcasted_iota(jnp.int32, (nodes, nodes), 1))
+        counts = jnp.sum(jnp.where(across, count_ref[...].astype(F32), 0.0), axis=1, keepdims=True)
+        slot_id = lax.broadcasted_iota(jnp.int32, recv_ref.shape, 1).astype(F32)
+        live = jnp.where(slot_id < counts, recv_ref[...], -1)
+        for q in range(NZ):
+            recv_live[q] = live[q * NY:(q + 1) * NY]
+        lax.fori_loop(0, NZ, build_place, 0)
+        degree[...] = jnp.ones_like(degree)
+        total[...] = x_ref[...].astype(F32)
+
+    if packed:
+        select_last(0, x_ref)
+        ov, ov_t = prepare()
+        start_hops(0)
+
+        def middle():
+            prepare_unpack(ov, ov_t)
+            prepare_place()
+
+        finish_packed(0, middle)
+    else:
+        prepare_place()
+        add_near(0)
+        add_far(0, 0, 5)
+        pass_w1()
+        add_far(0, 5, 7)
     degree[...] = 1.0 / degree[...]
-
-    total[...] = x_ref[...].astype(F32)
-    add_all(0, pass_w1)
     mine[...] = (total[...] * degree[...]).astype(BF16)
 
     piece = part // PIECES
@@ -229,16 +434,33 @@
 
     send_rest(1, second, 0)
     total[...] = second[...].astype(F32)
-    add_all(1)
+    if packed:
+        select_last(1, second)
+        start_hops(1)
+        finish_packed(1)
+    else:
+        add_near(1)
+        add_far(1, 0, 7)
     out_ref[...] = (total[...] * degree[...]).astype(BF16)
 
-    def sent(k, _):
-        other = lax.rem(node + k, NODES)
-        slot_copy(0, other).wait_send()
-        slot_copy(1, other).wait_send()
+    def sent(i, _):
+        for j in range(NY):
+            for layer in range(2):
+                slot_copy(layer, near(i) * NY + j, base).wait_send()
+            if packed:
+                count_copy(near(i) * NY + j).wait_send()
         return 0
 
-    lax.fori_loop(1, NODES, sent, 0)
+    lax.fori_loop(0, NZ - 1, sent, 0)
+    for j in range(1, NY):
+        other = z * NY + lax.rem(y + j, NY)
+        for layer in range(2):
+            slot_copy(layer, other, slots).wait_send()
+        if packed:
+            count_copy(other).wait_send()
+    if packed:
+        sent_hops(0)
+        sent_hops(1)
     for dx in range(1, NX):
         w1_copy(dx).wait_send()
     for dx in range(NX):
@@ -249,45 +471,68 @@
             row_copy(1, h, d).wait_send()
 
 
-def per_device(batch_node_input, weight_in, second_layer_weight, send_rows, recv_rows, block_count):
+def layers(packed, batch_node_input, weight_in, second_layer_weight, send_rows, recv_rows, block_count):
     rows, width = batch_node_input.shape
     nodes, slots = send_rows.shape[1:]
     part = rows // FEATS
     hidden = weight_in.shape[1]
     vmem = pl.BlockSpec(memory_space=pltpu.VMEM)
     dma = pltpu.SemaphoreType.DMA
+    out_shape = [jax.ShapeDtypeStruct((rows, width), BF16)]
+    scratch = [
+        pltpu.VMEM((rows, width), BF16),
+        pltpu.VMEM((nodes, slots), jnp.int32),
+        pltpu.VMEM((nodes, slots), jnp.int32),
+        pltpu.VMEM((1, nodes), jnp.int32),
+        pltpu.VMEM((FEATS, width, hidden), BF16),
+        pltpu.VMEM((hidden, hidden), BF16),
+        pltpu.VMEM((2, nodes, slots, width), BF16),
+        pltpu.VMEM((2, nodes, slots, width), BF16),
+        pltpu.VMEM((slots, nodes), F32),
+        pltpu.VMEM((NZ, NY, slots), jnp.int32),
+        pltpu.VMEM((NZ, NY * slots, rows), BF16),
+        pltpu.VMEM((NZ, rows, NY * slots), BF16),
+        pltpu.VMEM((rows, width), F32),
+        pltpu.VMEM((rows, width), F32),
+        pltpu.VMEM((rows, width), BF16),
+        pltpu.VMEM((FEATS, part, width), BF16),
+        pltpu.VMEM((FEATS, part, width), BF16),
+        pltpu.VMEM((rows, width), BF16),
+        dma((2, nodes)), dma((2, nodes)),
+        dma((NX,)), dma((NX,)), dma((NX,)), dma((NX,)),
+        dma((2, PIECES, FEATS)), dma((2, PIECES, FEATS)),
+        dma((6,)),
+    ]
+    if packed:
+        rest = slots - BASE
+        out_shape.append(jax.ShapeDtypeStruct((8, 128), F32))
+        scratch += [
+            pltpu.VMEM((nodes, 1, nodes), jnp.int32),
+            pltpu.VMEM((nodes, 128), F32),
+            pltpu.VMEM((NZ, NY, slots), F32),
+            pltpu.VMEM((2, 4, CAPS[0], NY * slots), BF16),
+            *[pltpu.VMEM((2, NY * rest, cap), BF16) for cap in CAPS],
+            pltpu.VMEM((2, 2, CAPS[0], width), BF16),
+            *[pltpu.VMEM((2, 2, cap, width), BF16) for cap in CAPS],
+            pltpu.VMEM((2, 2, 4, NY, rest, width), BF16),
+            dma((nodes,)), dma((nodes,)),
+            dma((2, 2, 4)), dma((2, 2, 4)),
+            dma((2, 2, 4, NY)), dma((2, nodes)),
+        ]
     return pl.pallas_call(
-        kernel,
-        out_shape=jax.ShapeDtypeStruct((rows, width), BF16),
+        functools.partial(kernel, packed),
+        out_shape=out_shape,
         in_specs=[pl.BlockSpec(memory_space=pltpu.HBM)] * 6,
-        out_specs=vmem,
-        scratch_shapes=[
-            pltpu.VMEM((rows, width), BF16),
-            pltpu.VMEM((nodes, slots), jnp.int32),
-            pltpu.VMEM((nodes, slots), jnp.int32),
-            pltpu.VMEM((1, nodes), jnp.int32),
-            pltpu.VMEM((FEATS, width, hidden), BF16),
-            pltpu.VMEM((hidden, hidden), BF16),
-            pltpu.VMEM((2, nodes, slots, width), BF16),
-            pltpu.VMEM((2, nodes, slots, width), BF16),
-            pltpu.VMEM((slots, nodes), F32),
-            pltpu.VMEM((NZ, NY, slots), jnp.int32),
-            pltpu.VMEM((NZ, NY * slots, rows), BF16),
-            pltpu.VMEM((NZ, rows, NY * slots), BF16),
-            pltpu.VMEM((rows, width), F32),
-            pltpu.VMEM((rows, width), F32),
-            pltpu.VMEM((rows, width), BF16),
-            pltpu.VMEM((FEATS, part, width), BF16),
-            pltpu.VMEM((FEATS, part, width), BF16),
-            pltpu.VMEM((rows, width), BF16),
-            dma((2, nodes)), dma((2, nodes)),
-            dma((NX,)), dma((NX,)), dma((NX,)), dma((NX,)),
-            dma((2, PIECES, FEATS)), dma((2, PIECES, FEATS)),
-            dma((6,)),
-        ],
+        out_specs=[vmem] * len(out_shape),
+        scratch_shapes=scratch,
         compiler_params=pltpu.CompilerParams(
-            collective_id=0, has_side_effects=True, vmem_limit_bytes=60 * 2**20),
+            collective_id=0 if packed else 1, has_side_effects=True, vmem_limit_bytes=60 * 2**20),
     )(batch_node_input, weight_in, second_layer_weight, send_rows[0], recv_rows[0], block_count[:, :, 0])
+
+
+def per_device(*args):
+    result, over = layers(True, *args)
+    return lax.cond(over[0, 0] > 0.0, lambda: layers(False, *args)[0], lambda: result)
 
 
 def solution(mesh):

time: 81 us -> 85.8 us (1.059)
  the two profiles are of different devices: /device:TPU:40 before, /device:TPU:32 now
where the time goes in v5:
time: 85.8 us; the launch traced here: 85 us
  Pallas kernels  82.1 us (96%)
  local copies, waits for them, and re-layouts  1.97 us (2%)
    pallas_call x1, Pallas kernels, layers(): pl.pallas_call(functools.partial(kernel, packed), out_shape=out_shape, in...  82.1 us

profile of v5, /device:TPU:32, one launch (start us, length us, event | category | flops | bytes accessed | tf_op | source)
XLA Modules:
  0.0 85.0 jit_solution(11145534711117153072)
XLA Ops:
  0.0 0.0 copy-start.5
  0.0 0.0 copy-start.4
  0.0 0.0 copy-start.3
  0.0 0.0 copy-start
  0.0 0.0 copy-start.2
  0.0 0.0 copy-start.1
  0.0 82.1 %shard_map.66 = (bf16[1536,128]{1,0:T(8,128)(2,1)S(1)}, f32[8,128]{1,0:T(8,128)}) custom-call(bf16[1536,128]{1,0:T(8,128)(2,1)} %x_hbm.1, bf16[128,1024]{1,0:T(8,128)(2,1)} %w1_hbm.1, bf16[1024,1024]{1,0:T(8,128)(2,1)} %w2_hbm.1, s32[32,128]{1,0:T(8,128)} %bitcast.7, s32[32,128]{1,0:T(8,128)} %bitcast.9, s32[1,32]{1,0:T(1,128)} %bitcast.11), custom_call_target="tpu_custom_call" | custom-call | tf_op jit(solution)/shard_map/pallas_call | solution.py:522
  82.1 1.2 %slice.3 = f32[1,1]{1,0:T(1,128)} slice(f32[8,128]{1,0:T(8,128)} %get-tuple-element.29), slice={[0:1], [0:1]} | slice | bytes 8 | tf_op jit(solution)/shard_map/slice | solution.py:535
  84.0 0.0 copy-done.5
  84.0 0.0 copy-done.4
  84.0 0.0 copy-done.3
  84.0 0.0 copy-done
  84.0 0.0 copy-done.2
  84.0 0.0 copy-done.1
  84.0 0.2 conditional.1
  84.3 0.7 copy.12
Async XLA Ops:
  0.0 84.0 %copy-start.5 = (s32[1,32,1]{1,2,0:T(1,128)S(1)}, s32[1,32,1]{1,2,0:T(1,128)}, u32[]{:S(2)}) copy-start(s32[1,32,1]{1,2,0:T(1,128)} %param.13) | copy-start | bytes 388
  0.0 84.0 %copy-start.4 = (s32[1,32,128]{2,1,0:T(8,128)S(1)}, s32[1,32,128]{2,1,0:T(8,128)}, u32[]{:S(2)}) copy-start(s32[1,32,128]{2,1,0:T(8,128)} %param.12) | copy-start | bytes 49156
  0.0 84.0 %copy-start.3 = (s32[1,32,128]{2,1,0:T(8,128)S(1)}, s32[1,32,128]{2,1,0:T(8,128)}, u32[]{:S(2)}) copy-start(s32[1,32,128]{2,1,0:T(8,128)} %param.11) | copy-start | bytes 49156
  0.0 84.0 %copy-start = (bf16[1024,1024]{1,0:T(8,128)(2,1)S(1)}, bf16[1024,1024]{1,0:T(8,128)(2,1)}, u32[]{:S(2)}) copy-start(bf16[1024,1024]{1,0:T(8,128)(2,1)} %w2_hbm.1) | copy-start | bytes 6291460
  0.0 84.0 %copy-start.2 = (bf16[128,1024]{1,0:T(8,128)(2,1)S(1)}, bf16[128,1024]{1,0:T(8,128)(2,1)}, u32[]{:S(2)}) copy-start(bf16[128,1024]{1,0:T(8,128)(2,1)} %w1_hbm.1) | copy-start | bytes 786436
  0.0 84.0 %copy-start.1 = (bf16[1536,128]{1,0:T(8,128)(2,1)S(1)}, bf16[1536,128]{1,0:T(8,128)(2,1)}, u32[]{:S(2)}) copy-start(bf16[1536,128]{1,0:T(8,128)(2,1)} %x_hbm.1) | copy-start | bytes 1179652

commit v6 on v4

v6 whole, which is shorter than its diff:
```python
import functools

import jax
import jax.numpy as jnp
from jax import lax
from jax.experimental import pallas as pl
from jax.experimental.pallas import tpu as pltpu
from jax.sharding import PartitionSpec as P

MESH = pl.DeviceIdType.MESH
NZ, NY, NX, NC = 8, 4, 4, 2
NODES, FEATS = NZ * NY, NX * NC
PIECES = 2
FEAT_STEPS = ((2, 0), (2, 1), (1, 0), (3, 0), (1, 1), (3, 1), (0, 1))
BF16, F32 = jnp.bfloat16, jnp.float32


def order(i):
    return lax.rem(4 + lax.rem(i, 2) * ((i + 1) // 2) - (1 - lax.rem(i, 2)) * (i // 2), NZ)


def swap(v):
    half = v.shape[-1] // 2
    return jnp.concatenate([v[..., half:], v[..., :half]], axis=-1)


def low_lanes(v):
    return lax.broadcasted_iota(jnp.int32, v.shape, v.ndim - 1) < v.shape[-1] // 2


def join(a, b):
    return jnp.where(low_lanes(a), a, swap(b))


def join_high(a, b):
    return jnp.where(low_lanes(a), swap(a), b)


def pair(first, later, half):
    return join(first, later) if half == 0 else join_high(later, first)


def kernel(
    x_hbm, w1_hbm, w2_hbm, send_hbm, recv_hbm, count_hbm, out_ref,
    x_ref, send_ref, recv_ref, count_ref, w1_all, w2_all, out_slots, in_slots, send_cols, recv_live, pick, place,
    total, degree, mine, rows_in, rows_out, back, second, before,
    slot_send, slot_recv, w1_send, w1_recv, w1_send2, w1_recv2, row_send, row_recv, in_sem,
):
    rows, width = x_ref.shape
    slots = send_ref.shape[1]
    part = rows // FEATS
    near_slots = slots // 2
    node, feat = lax.axis_index("node"), lax.axis_index("feat")
    z, y = node // NY, lax.rem(node, NY)
    x, c = feat // NC, lax.rem(feat, NC)

    barrier = pltpu.get_barrier_semaphore()

    def greet_plane(i, _):
        zz = lax.rem(z + order(i), NZ)
        for j in range(NY):
            pl.semaphore_signal(barrier, inc=1, device_id=(zz * NY + j, feat), device_id_type=MESH)
        return 0

    lax.fori_loop(0, NZ - 1, greet_plane, 0)
    for j in range(1, NY):
        pl.semaphore_signal(
            barrier, inc=1, device_id=(z * NY + lax.rem(y + j, NY), feat), device_id_type=MESH)
    for d in range(1, FEATS):
        pl.semaphore_signal(
            barrier, inc=1, device_id=(node, lax.rem(feat + d, FEATS)), device_id_type=MESH)

    send_in = pltpu.make_async_copy(send_hbm, send_ref, in_sem.at[0])
    x_in = pltpu.make_async_copy(x_hbm, x_ref, in_sem.at[1])
    recv_in = pltpu.make_async_copy(recv_hbm, recv_ref, in_sem.at[2])
    count_in = pltpu.make_async_copy(count_hbm, count_ref, in_sem.at[3])
    w1_in = pltpu.make_async_copy(w1_hbm, w1_all.at[feat], in_sem.at[4])
    w2_in = pltpu.make_async_copy(w2_hbm, w2_all, in_sem.at[5])
    for copy in (send_in, x_in, recv_in, count_in, w1_in, w2_in):
        copy.start()

    def w1_copy(dx):
        return pltpu.make_async_remote_copy(
            w1_hbm, w1_all.at[feat], w1_send.at[dx], w1_recv.at[dx],
            device_id=(node, lax.rem(x + dx, NX) * NC + c), device_id_type=MESH)

    def w1_pass(dx):
        held = lax.rem(x + NX - dx, NX) * NC + c
        return pltpu.make_async_remote_copy(
            w1_hbm if dx == 0 else w1_all.at[held], w1_all.at[held], w1_send2.at[dx], w1_recv2.at[dx],
            device_id=(node, x * NC + 1 - c), device_id_type=MESH)

    def slot_copy(layer, half, other):
        k = 2 * layer + half
        return pltpu.make_async_remote_copy(
            out_slots.at[k, other], in_slots.at[k, node], slot_send.at[k, other], slot_recv.at[k, node],
            device_id=(other, feat), device_id_type=MESH)

    def slot_wait(layer, half, other):
        k = 2 * layer + half
        pltpu.make_async_remote_copy(
            out_slots.at[k, other], in_slots.at[k, other], slot_send.at[k, other], slot_recv.at[k, other],
            device_id=(other, feat), device_id_type=MESH).wait_recv()

    def build_pick(zz):
        cols = send_cols[...]
        lane = lax.broadcasted_iota(jnp.int32, cols.shape, 1)
        row_id = lax.broadcasted_iota(jnp.int32, (slots, rows), 1).astype(F32)
        for j in range(NY):
            col = jnp.sum(jnp.where(lane == zz * NY + j, cols, 0.0), axis=1, keepdims=True)
            hot = jnp.where(row_id == col, 1.0, 0.0).astype(BF16)
            for k in range(2):
                at = (k * NY + j) * near_slots
                pick[zz, at:at + near_slots, :] = hot[k * near_slots:(k + 1) * near_slots]

    def select(layer, halves, source, zz):
        if layer == 0:
            build_pick(zz)
        got = jnp.dot(pick[zz], source, preferred_element_type=F32).astype(BF16)
        for half in halves:
            packed = pair(got[:NY * near_slots], got[NY * near_slots:], half)
            out_slots[2 * layer + half, pl.ds(zz * NY, NY)] = packed.reshape(NY, near_slots, width)

    def send_plane(layer, half, zz):
        for j in (2, 1, 3, 0):
            slot_copy(layer, half, zz * NY + lax.rem(y + j, NY)).start()

    def near(i):
        return lax.rem(z + order(NZ - 2 - i), NZ)

    def send_own(layer, half):
        for j in (2, 1, 3):
            slot_copy(layer, half, z * NY + lax.rem(y + j, NY)).start()
        in_slots[2 * layer + half, node] = out_slots[2 * layer + half, node]

    def send_half(layer, half, halves, source, first):
        def plane(i, _):
            if halves:
                select(layer, halves, source[...], near(i))
            send_plane(layer, half, near(i))
            return 0

        lax.fori_loop(first, NZ - 1, plane, 0)
        if halves:
            select(layer, halves, source[...], z)
        send_own(layer, half)

    def build_place(zz, _):
        ids = recv_live[zz]
        row_id = lax.broadcasted_iota(jnp.int32, (rows, slots), 0)
        for j in range(NY):
            place[zz, :, j * slots:(j + 1) * slots] = jnp.where(
                row_id == ids[:, j * slots:(j + 1) * slots], 1.0, 0.0).astype(BF16)
        degree[...] += jnp.dot(
            place[zz], jnp.ones((NY * slots, width), BF16), preferred_element_type=F32)
        return 0

    def add_plane(layer, half, zz):
        held = in_slots[2 * layer + half, pl.ds(zz * NY, NY)].reshape(NY * near_slots, width)
        held = jnp.concatenate([held, swap(held)], axis=0)
        total[half] += jnp.dot(place[zz], held, preferred_element_type=F32)

    def add_own(layer, half):
        for j in range(1, NY):
            slot_wait(layer, half, z * NY + lax.rem(y + j, NY))
        add_plane(layer, half, z)

    def add_far(layer, half, first, last):
        def plane(i, _):
            zz = lax.rem(z + NZ - order(NZ - 2 - i), NZ)
            for j in range(NY):
                slot_wait(layer, half, zz * NY + j)
            add_plane(layer, half, zz)
            return 0

        lax.fori_loop(first, last, plane, 0)

    def pass_w1():
        for dx in range(1, NX):
            w1_copy(dx).wait_recv()
            w1_pass(dx).start()

    early = 2
    send_in.wait()
    send_cols[...] = send_ref[...].astype(F32).T
    x_in.wait()
    for i in range(early):
        select(0, (0, 1), x_ref[...], near(i))

    pl.semaphore_wait(barrier, NODES + FEATS - 2)

    for i in range(early):
        send_plane(0, 0, near(i))
    for dx in range(1, NX):
        w1_copy(dx).start()
    w1_pass(0).start()

    send_half(0, 0, (0, 1), x_ref, early)
    send_half(0, 1, (), x_ref, 0)

    recv_in.wait()
    count_in.wait()
    nodes = recv_ref.shape[0]
    across = (lax.broadcasted_iota(jnp.int32, (nodes, nodes), 0)
              == lax.broadcasted_iota(jnp.int32, (nodes, nodes), 1))
    counts = jnp.sum(jnp.where(across, count_ref[...].astype(F32), 0.0), axis=1, keepdims=True)
    slot_id = lax.broadcasted_iota(jnp.int32, recv_ref.shape, 1).astype(F32)
    live = jnp.where(slot_id < counts, recv_ref[...], -1)
    for q in range(NZ):
        blocks = [live[q * NY + j:q * NY + j + 1] for j in range(NY)]
        recv_live[q] = jnp.concatenate(
            [b[:, :near_slots] for b in blocks] + [b[:, near_slots:] for b in blocks], axis=1)
    degree[...] = jnp.ones_like(degree)
    lax.fori_loop(0, NZ, build_place, 0)
    degree[...] = 1.0 / degree[...]

    low = part // 2
    piece = low // PIECES

    def row_copy(step, half, h, d):
        dx, dc = FEAT_STEPS[d]
        other = lax.rem(x + dx, NX) * NC + lax.rem(c + dc, NC)
        source = (mine if step == 0 else rows_out).at[half, other, pl.ds(h * piece, piece)]
        target = (rows_in if step == 0 else back).at[half, feat, pl.ds(h * piece, piece)]
        k = 2 * step + half
        return pltpu.make_async_remote_copy(
            source, target, row_send.at[k, h, d], row_recv.at[k, h, d],
            device_id=(node, other), device_id_type=MESH)

    each = range(len(FEAT_STEPS))

    def send_rows(half):
        scaled = (total[half] * degree[...]).astype(BF16)
        for f in range(FEATS):
            mine[half, f] = pair(scaled[f * part:f * part + low], scaled[f * part + low:(f + 1) * part], half)
        for h in range(PIECES):
            for d in each:
                row_copy(0, half, h, d).start()
        rows_in[half, feat] = mine[half, feat]

    def multiply(half, h):
        got = [rows_in[half, f, h * piece:(h + 1) * piece] for f in range(FEATS)]
        pairs = [(got[f], got[f + 1]) for f in range(0, FEATS, 2)]
        lows = jnp.concatenate([join(*p) for p in pairs], axis=1)
        highs = jnp.concatenate([join_high(*p) for p in pairs], axis=1)
        held = jnp.concatenate([lows, highs] if half == 0 else [highs, lows], axis=0)
        span = slice(0, width // 2) if half == 0 else slice(width // 2, width)
        weight = w1_all[:, span, :].reshape(FEATS * width // 2, FEATS * width)
        return jnp.dot(held, weight, preferred_element_type=F32)

    for half in range(2):
        total[half] = x_ref[...].astype(F32)
    add_own(0, 0)
    add_far(0, 0, 0, 5)
    pass_w1()
    add_far(0, 0, 5, 7)
    send_rows(0)
    add_own(0, 1)
    add_far(0, 1, 0, 4)
    for dx in range(NX):
        w1_pass(dx).wait_recv()
    w1_in.wait()
    w2_in.wait()
    for h in range(PIECES):
        for d in each:
            row_copy(0, 0, h, d).wait_recv()
        before[h] = multiply(0, h)
    add_far(0, 1, 4, 7)
    send_rows(1)
    for h in range(PIECES):
        for d in each:
            row_copy(0, 1, h, d).wait_recv()
        hidden = jnp.maximum(before[h] + multiply(1, h), 0.0).astype(BF16)
        result = jnp.dot(hidden, w2_all[...], preferred_element_type=F32).astype(BF16)
        for half in range(2):
            for f in range(FEATS):
                block = result[:, f * width:(f + 1) * width]
                rows_out[half, f, h * piece:(h + 1) * piece] = pair(block[:piece], block[piece:], half)
        for d in each:
            row_copy(1, 0, h, d).start()
    for h in range(PIECES):
        for d in each:
            row_copy(1, 1, h, d).start()

    for half in range(2):
        back[half, feat] = rows_out[half, feat]
        for h in range(PIECES):
            for d in each:
                row_copy(1, half, h, d).wait_recv()
        for f in range(FEATS):
            got = back[half, f]
            second[half, f * part:f * part + low] = got
            second[half, f * part + low:(f + 1) * part] = swap(got)
        send_half(1, half, (half,), second.at[half], 0)
    for half in range(2):
        total[half] = second[half].astype(F32)
        add_own(1, half)
        add_far(1, half, 0, 7)
    out_ref[...] = (jnp.where(low_lanes(total[0]), total[0], total[1]) * degree[...]).astype(BF16)

    def sent(k, _):
        other = lax.rem(node + k, NODES)
        for layer in range(2):
            for half in range(2):
                slot_copy(layer, half, other).wait_send()
        return 0

    lax.fori_loop(1, NODES, sent, 0)
    for dx in range(1, NX):
        w1_copy(dx).wait_send()
    for dx in range(NX):
        w1_pass(dx).wait_send()
    for h in range(PIECES):
        for d in each:
            for step in range(2):
                for half in range(2):
                    row_copy(step, half, h, d).wait_send()


def per_device(batch_node_input, weight_in, second_layer_weight, send_rows, recv_rows, block_count):
    rows, width = batch_node_input.shape
    nodes, slots = send_rows.shape[1:]
    part = rows // FEATS
    hidden = weight_in.shape[1]
    vmem = pl.BlockSpec(memory_space=pltpu.VMEM)
    dma = pltpu.SemaphoreType.DMA
    return pl.pallas_call(
        kernel,
        out_shape=jax.ShapeDtypeStruct((rows, width), BF16),
        in_specs=[pl.BlockSpec(memory_space=pltpu.HBM)] * 6,
        out_specs=vmem,
        scratch_shapes=[
            pltpu.VMEM((rows, width), BF16),
            pltpu.VMEM((nodes, slots), jnp.int32),
            pltpu.VMEM((nodes, slots), jnp.int32),
            pltpu.VMEM((1, nodes), jnp.int32),
            pltpu.VMEM((FEATS, width, hidden), BF16),
            pltpu.VMEM((hidden, hidden), BF16),
            pltpu.VMEM((4, nodes, slots // 2, width), BF16),
            pltpu.VMEM((4, nodes, slots // 2, width), BF16),
            pltpu.VMEM((slots, nodes), F32),
            pltpu.VMEM((NZ, 1, NY * slots), jnp.int32),
            pltpu.VMEM((NZ, NY * slots, rows), BF16),
            pltpu.VMEM((NZ, rows, NY * slots), BF16),
            pltpu.VMEM((2, rows, width), F32),
            pltpu.VMEM((rows, width), F32),
            pltpu.VMEM((2, FEATS, part // 2, width), BF16),
            pltpu.VMEM((2, FEATS, part // 2, width), BF16),
            pltpu.VMEM((2, FEATS, part // 2, width), BF16),
            pltpu.VMEM((2, FEATS, part // 2, width), BF16),
            pltpu.VMEM((2, rows, width), BF16),
            pltpu.VMEM((PIECES, part // PIECES, hidden), F32),
            dma((4, nodes)), dma((4, nodes)),
            dma((NX,)), dma((NX,)), dma((NX,)), dma((NX,)),
            dma((4, PIECES, FEATS)), dma((4, PIECES, FEATS)),
            dma((6,)),
        ],
        compiler_params=pltpu.CompilerParams(
            collective_id=0, has_side_effects=True, vmem_limit_bytes=60 * 2**20),
    )(batch_node_input, weight_in, second_layer_weight, send_rows[0], recv_rows[0], block_count[:, :, 0])


def solution(mesh):
    return jax.shard_map(
        per_device, mesh=mesh,
        in_specs=(P("node", "feat"), P("feat", None), P(), P("node", None, None), P("node", None, None), P("node", None, None)),
        out_specs=P("node", "feat"), check_vma=False)
```

time: 81 us -> 83.7 us (1.033)
  the two profiles are of different devices: /device:TPU:40 before, /device:TPU:32 now
where the time goes in v6:
time: 83.7 us; the launch traced here: 82.6 us
  Pallas kernels  80.8 us (97%)
  local copies, waits for them, and re-layouts  1.77 us (2%)
    pallas_call x1, Pallas kernels, per_device(): pl.pallas_call(kernel, out_shape=jax.ShapeDtypeStruct((rows, width), BF16...  80.8 us
    unnamed x1, local copies, waits for them, and re-layouts  1.77 us

profile of v6, /device:TPU:32, one launch (start us, length us, event | category | flops | bytes accessed | tf_op | source)
XLA Modules:
  0.0 82.6 jit_solution(6959803201793996295)
XLA Ops:
  0.0 80.8 %shard_map.64 = bf16[1536,128]{1,0:T(8,128)(2,1)} custom-call(bf16[1536,128]{1,0:T(8,128)(2,1)} %x_hbm.1, bf16[128,1024]{1,0:T(8,128)(2,1)} %w1_hbm.1, bf16[1024,1024]{1,0:T(8,128)(2,1)} %w2_hbm.1, s32[32,128]{1,0:T(8,128)} %bitcast.3, s32[32,128]{1,0:T(8,128)} %bitcast.4, s32[1,32]{1,0:T(1,128)} %bitcast.5), custom_call_target="tpu_custom_call" | custom-call | tf_op jit(solution)/shard_map/pallas_call | solution.py:327
  80.8 1.8 %copy.8 = bf16[1536,128]{1,0:T(8,128)(2,1)} copy(bf16[1536,128]{1,0:T(8,128)(2,1)} %shard_map.64) | data formatting | bytes 786432

commit v7 on v4

--- a/solution.py
+++ b/solution.py
@@ -10,8 +10,8 @@
 MESH = pl.DeviceIdType.MESH
 NZ, NY, NX, NC = 8, 4, 4, 2
 NODES, FEATS = NZ * NY, NX * NC
-PIECES = 2
-FEAT_STEPS = ((2, 0), (2, 1), (1, 0), (3, 0), (1, 1), (3, 1), (0, 1))
+PIECES = 1
+FEAT_STEPS = ((2, 1), (1, 1), (3, 1), (2, 0), (1, 0), (3, 0), (0, 1))
 BF16, F32 = jnp.bfloat16, jnp.float32
 
 
@@ -95,8 +95,8 @@
         out_slots[layer, pl.ds(zz * NY, NY)] = got.reshape(NY, slots, width)
 
     def send_plane(layer, zz):
-        for j in range(NY):
-            slot_copy(layer, zz * NY + j).start()
+        for j in (2, 1, 3, 0):
+            slot_copy(layer, zz * NY + lax.rem(y + j, NY)).start()
 
     def near(i):
         return lax.rem(z + order(NZ - 2 - i), NZ)

time: 81 us -> 79.5 us (0.981)
  the two profiles are of different devices: /device:TPU:40 before, /device:TPU:32 now
where the time goes in v7:
time: 79.5 us; the launch traced here: 79.3 us
  Pallas kernels  77.5 us (97%)
  local copies, waits for them, and re-layouts  1.77 us (2%)
    pallas_call x1, Pallas kernels, per_device(): pl.pallas_call(kernel, out_shape=jax.ShapeDtypeStruct((rows, width), BF16...  77.5 us
    unnamed x1, local copies, waits for them, and re-layouts  1.77 us

profile of v7, /device:TPU:32, one launch (start us, length us, event | category | flops | bytes accessed | tf_op | source)
XLA Modules:
  0.0 79.3 jit_solution(480990837097042183)
XLA Ops:
  0.0 77.5 %shard_map.64 = bf16[1536,128]{1,0:T(8,128)(2,1)} custom-call(bf16[1536,128]{1,0:T(8,128)(2,1)} %x_hbm.1, bf16[128,1024]{1,0:T(8,128)(2,1)} %w1_hbm.1, bf16[1024,1024]{1,0:T(8,128)(2,1)} %w2_hbm.1, s32[32,128]{1,0:T(8,128)} %bitcast.3, s32[32,128]{1,0:T(8,128)} %bitcast.4, s32[1,32]{1,0:T(1,128)} %bitcast.5), custom_call_target="tpu_custom_call" | custom-call | tf_op jit(solution)/shard_map/pallas_call | solution.py:259
  77.5 1.8 %copy.8 = bf16[1536,128]{1,0:T(8,128)(2,1)} copy(bf16[1536,128]{1,0:T(8,128)(2,1)} %shard_map.64) | data formatting | bytes 786432

commit v8 on v7

--- a/solution.py
+++ b/solution.py
@@ -99,7 +99,7 @@
             slot_copy(layer, zz * NY + lax.rem(y + j, NY)).start()
 
     def near(i):
-        return lax.rem(z + order(NZ - 2 - i), NZ)
+        return lax.rem(z + order(NZ - 2 - lax.rem(i + 2, NZ - 1)), NZ)
 
     def send_rest(layer, source, first):
         def plane(i, _):
@@ -133,7 +133,7 @@
         add_plane(layer, z)
 
         def plane(i, _):
-            zz = lax.rem(z + NZ - order(NZ - 2 - i), NZ)
+            zz = lax.rem(z + NZ - order(NZ - 2 - lax.rem(i + 2, NZ - 1)), NZ)
             for j in range(NY):
                 slot_wait(layer, zz * NY + j)
             add_plane(layer, zz)

time: 79.5 us -> 78.6 us (0.989)
  Pallas kernels: 77.5 us -> 76.7 us
    pallas_call x1, Pallas kernels: 77.5 us -> 76.7 us  [per_device(): pl.pallas_call(kernel, out_shape=jax.ShapeDtypeStruct((rows, width), BF16...]
where the time goes in v8:
time: 78.6 us; the launch traced here: 78.5 us
  Pallas kernels  76.7 us (98%)
  local copies, waits for them, and re-layouts  1.77 us (2%)
    pallas_call x1, Pallas kernels, per_device(): pl.pallas_call(kernel, out_shape=jax.ShapeDtypeStruct((rows, width), BF16...  76.7 us
    unnamed x1, local copies, waits for them, and re-layouts  1.77 us

profile of v8, /device:TPU:32, one launch (start us, length us, event | category | flops | bytes accessed | tf_op | source)
XLA Modules:
  0.0 78.5 jit_solution(2770067019018707527)
XLA Ops:
  0.0 76.7 %shard_map.64 = bf16[1536,128]{1,0:T(8,128)(2,1)} custom-call(bf16[1536,128]{1,0:T(8,128)(2,1)} %x_hbm.1, bf16[128,1024]{1,0:T(8,128)(2,1)} %w1_hbm.1, bf16[1024,1024]{1,0:T(8,128)(2,1)} %w2_hbm.1, s32[32,128]{1,0:T(8,128)} %bitcast.3, s32[32,128]{1,0:T(8,128)} %bitcast.4, s32[1,32]{1,0:T(1,128)} %bitcast.5), custom_call_target="tpu_custom_call" | custom-call | tf_op jit(solution)/shard_map/pallas_call | solution.py:259
  76.7 1.8 %copy.8 = bf16[1536,128]{1,0:T(8,128)(2,1)} copy(bf16[1536,128]{1,0:T(8,128)(2,1)} %shard_map.64) | data formatting | bytes 786432

commit v9 on v8

--- a/solution.py
+++ b/solution.py
@@ -107,11 +107,12 @@
             send_plane(layer, near(i))
             return 0
 
-        lax.fori_loop(first, NZ - 1, plane, 0)
+        lax.fori_loop(first, NZ - 3, plane, 0)
         select(layer, source, z)
         for j in range(1, NY):
             slot_copy(layer, z * NY + lax.rem(y + j, NY)).start()
         in_slots[layer, node] = out_slots[layer, node]
+        lax.fori_loop(NZ - 3, NZ - 1, plane, 0)
 
     def build_place(zz, _):
         ids = recv_live[zz]
@@ -128,10 +129,6 @@
         total[...] += jnp.dot(place[zz], held, preferred_element_type=F32)
 
     def add_all(layer, middle=None):
-        for j in range(1, NY):
-            slot_wait(layer, z * NY + lax.rem(y + j, NY))
-        add_plane(layer, z)
-
         def plane(i, _):
             zz = lax.rem(z + NZ - order(NZ - 2 - lax.rem(i + 2, NZ - 1)), NZ)
             for j in range(NY):
@@ -139,12 +136,13 @@
             add_plane(layer, zz)
             return 0
 
-        if middle is None:
-            lax.fori_loop(0, NZ - 1, plane, 0)
-        else:
-            lax.fori_loop(0, NZ - 3, plane, 0)
+        lax.fori_loop(0, NZ - 3, plane, 0)
+        if middle is not None:
             middle()
-            lax.fori_loop(NZ - 3, NZ - 1, plane, 0)
+        for j in range(1, NY):
+            slot_wait(layer, z * NY + lax.rem(y + j, NY))
+        add_plane(layer, z)
+        lax.fori_loop(NZ - 3, NZ - 1, plane, 0)
 
     def pass_w1():
         for dx in range(1, NX):

time: 78.6 us -> 79.5 us (1.011)
  Pallas kernels: 76.7 us -> 77.6 us
    pallas_call x1, Pallas kernels: 76.7 us -> 77.6 us  [per_device(): pl.pallas_call(kernel, out_shape=jax.ShapeDtypeStruct((rows, width), BF16...]
where the time goes in v9:
time: 79.5 us; the launch traced here: 79.3 us
  Pallas kernels  77.6 us (98%)
  local copies, waits for them, and re-layouts  1.77 us (2%)
    pallas_call x1, Pallas kernels, per_device(): pl.pallas_call(kernel, out_shape=jax.ShapeDtypeStruct((rows, width), BF16...  77.6 us
    unnamed x1, local copies, waits for them, and re-layouts  1.77 us

profile of v9, /device:TPU:32, one launch (start us, length us, event | category | flops | bytes accessed | tf_op | source)
XLA Modules:
  0.0 79.3 jit_solution(8336535023176120385)
XLA Ops:
  0.0 77.6 %shard_map.64 = bf16[1536,128]{1,0:T(8,128)(2,1)} custom-call(bf16[1536,128]{1,0:T(8,128)(2,1)} %x_hbm.1, bf16[128,1024]{1,0:T(8,128)(2,1)} %w1_hbm.1, bf16[1024,1024]{1,0:T(8,128)(2,1)} %w2_hbm.1, s32[32,128]{1,0:T(8,128)} %bitcast.3, s32[32,128]{1,0:T(8,128)} %bitcast.4, s32[1,32]{1,0:T(1,128)} %bitcast.5), custom_call_target="tpu_custom_call" | custom-call | tf_op jit(solution)/shard_map/pallas_call | solution.py:257
  77.6 1.8 %copy.8 = bf16[1536,128]{1,0:T(8,128)(2,1)} copy(bf16[1536,128]{1,0:T(8,128)(2,1)} %shard_map.64) | data formatting | bytes 786432
